TPU v7x, 32 devices: a whole 2x2x4 slice. The times are simulated.
32 devices in a mesh: wave: 16 (over z, y, x), lev: 2 (over core).
Axes of the slice: x: 2, y: 2, z: 4, core: 2. Of those that a mesh axis runs over, the one named last changes fastest.
Arguments:
- fourier_in: bfloat16 [3, 28, 1280, 64], P(None, 'lev', 'wave'), may hold values from -6 to 6
- spectral_old: bfloat16 [3, 28, 16, 2816], P(None, 'lev', 'wave'), may hold values from -6 to 6
- legendre: bfloat16 [16, 1408, 1280], P('wave'), may hold values from -0.15625 to 0.15625
- g_matrix: float32 [28, 28], replicated, may hold values from -1 to 1
- modes_in: float32 [28, 28], replicated, may hold values from -1 to 1
- modes_out: float32 [28, 28], replicated, may hold values from -1 to 1
- mode_heating: float32 [28, 28], replicated, may hold values from -1 to 1
- mode_rates: float32 [28], replicated, may hold values from 0.1 to 10
- pair_ids: int32 [16], replicated, may hold values from 0 to 639, as said below
- lat_ids: int32 [1280], replicated, may hold values from 0 to 1279, each once
- limits: int32 [1280], replicated, may hold values from 10 to 1280
Outputs:
- spectral_new: bfloat16 [3, 28, 16, 2816], P(None, 'lev', 'wave')
- fourier_out: bfloat16 [3, 28, 1280, 64], P(None, 'lev', 'wave')
Inputs may be any that keep to these rules, and one draw needn't show every extreme that they name: `pair_ids`: distinct pair numbers. `lat_ids`: each latitude once.
All inputs are finite; a program needn't handle non-finite values.
Results may differ from a plain program's by a relative error of at most 0.018.
Values may be sent and summed in bfloat16 or wider, within the bound.
A program may use at most 64 MiB of HBM per device.

v0:
```python
import functools

import jax
import jax.numpy as jnp
from jax import lax
from jax.experimental import pallas as pl
from jax.experimental.pallas import tpu as pltpu
from jax.sharding import PartitionSpec as P

MMAX = 1280
BLOCK = 64
K = 4
F32, BF16 = jnp.float32, jnp.bfloat16
MESH = pl.DeviceIdType.MESH
HI = lax.Precision.HIGHEST
NT = (((1,), (1,)), ((), ()))


def iota(shape, dim):
    return lax.broadcasted_iota(jnp.int32, shape, dim)


def dot(a, b):
    return jnp.dot(a, b, preferred_element_type=F32)


def fdot(a, b):
    return jnp.dot(a, b, precision=HI, preferred_element_type=F32)


def onehot(mask, dtype=BF16):
    return jnp.where(mask, 1.0, 0.0).astype(dtype)


def split3(left, right):
    lh = left.astype(BF16)
    ll = (left - lh.astype(F32)).astype(BF16)
    rh = right.astype(BF16)
    rl = (right - rh.astype(F32)).astype(BF16)
    return jnp.concatenate([lh, lh, ll], axis=1), jnp.concatenate([rh, rl, rh], axis=0)


def kernel(
    n, nlev, x_hbm, old_hbm, leg_hbm, g_hbm, mi_hbm, mo_hbm, mh_hbm, rates_hbm, pid_hbm, lat_hbm, lim_hbm,
    spec_hbm, out_hbm,
    spec_ref, out_ref, x_ref, old_ref, leg, g_ref, mi_ref, mo_ref, mh_ref, rates_ref, pid_ref, lat_ref, lim_ref,
    send1, recv1, send2, recv2, es1, er1, es2, er2,
    out_sem, in_sem, s1, r1, s2, r2, es, er,
):
    lev_n = x_ref.shape[1]
    fl_n = x_ref.shape[0] * lev_n
    q_n, jl = x_ref.shape[2], x_ref.shape[3]
    groups = (fl_n + K - 1) // K
    rows = groups * 16
    trows = groups * 8
    lanes = send1.shape[2]
    nr = leg_hbm.shape[1]
    nlat = leg_hbm.shape[2]
    first_mid = lev_n // K * 8
    mid = trows - first_mid
    half = er1.shape[0]
    me, lev = lax.axis_index("wave"), lax.axis_index("lev")
    other = lax.rem(lev + 1, nlev)

    pairs = [
        (pid_hbm, pid_ref), (lat_hbm, lat_ref), (lim_hbm, lim_ref), (x_hbm, x_ref), (g_hbm, g_ref), (mi_hbm, mi_ref),
        (mo_hbm, mo_ref), (mh_hbm, mh_ref), (rates_hbm, rates_ref), (old_hbm, old_ref), (leg_hbm.at[0], leg),
    ]
    loads = [pltpu.make_async_copy(src, dst, in_sem.at[i]) for i, (src, dst) in enumerate(pairs)]
    for load in loads:
        load.start()

    barrier = pltpu.get_barrier_semaphore()

    def greet(i, carry):
        pl.semaphore_signal(barrier, inc=1, device_id=(lax.rem(me + i, n), lev), device_id_type=MESH)
        return carry

    lax.fori_loop(1, n, greet, 0)
    pl.semaphore_signal(barrier, inc=1, device_id=(me, other), device_id_type=MESH)

    for load in loads[:4]:
        load.wait()

    col = iota((jl, nlat), 1)
    own = jnp.sum(jnp.where(col == me * jl + iota((jl, nlat), 0), lat_ref[...].astype(F32)[None, :], 0.0), axis=1, keepdims=True)
    lim = jnp.sum(jnp.where(col.astype(F32) == own, lim_ref[...].astype(F32)[None, :], 0.0), axis=1, keepdims=True)
    lim = jnp.sum(jnp.where(iota((jl, jl), 0) == iota((jl, jl), 1), lim, 0.0), axis=0, keepdims=True)
    q = iota((q_n, jl), 0)
    slot = q // 4
    pair = jnp.zeros((q_n, jl), jnp.int32)
    for s in range(n):
        pair = jnp.where(slot == s, pid_ref[s], pair)
    wave = jnp.where(q // 2 % 2 == 0, pair, MMAX - 1 - pair)
    keep = onehot(wave.astype(F32) < lim, F32)

    pr, pc = iota((K * q_n, K * q_n), 0), iota((K * q_n, K * q_n), 1)
    perm = onehot(pc == pr % K * q_n + pr // K)
    keep_b = keep.astype(BF16)
    pieces = []
    for k in range(K):
        parts = []
        for g in range(groups):
            fl = g * K + k
            if fl < fl_n:
                parts.append(x_ref[fl // lev_n, fl % lev_n] * keep_b)
            else:
                parts.append(jnp.zeros((q_n, jl), BF16))
        if lanes > groups * jl:
            parts.append(jnp.zeros((q_n, lanes - groups * jl), BF16))
        pieces.append(jnp.concatenate(parts, axis=1))
    send1[...] = dot(perm, jnp.concatenate(pieces, axis=0)).astype(BF16).reshape(n, 16, lanes)

    pl.semaphore_wait(barrier, n)

    def copy1(i):
        to = lax.rem(me + i, n)
        return pltpu.make_async_remote_copy(
            src_ref=send1.at[to], dst_ref=recv1.at[me], send_sem=s1.at[to], recv_sem=r1.at[me],
            device_id=(to, lev), device_id_type=MESH,
        )

    def start1(i, carry):
        copy1(i).start()
        return carry

    lax.fori_loop(1, n, start1, 0)
    recv1[me] = send1[me]

    for load in loads[4:10]:
        load.wait()
    a = pid_ref[me]
    r = iota((1, nr), 1)
    first_pad = (MMAX - a + BLOCK - 1) // BLOCK * BLOCK
    first = r < first_pad
    used = (first & (r < MMAX - a)) | ((r >= first_pad) & (r - first_pad <= a))
    degree = jnp.where(first, a + r, MMAX - 1 - a + r - first_pad).astype(F32)
    lam = degree * (degree + 1.0) / float(MMAX * (MMAX - 1))

    tr, tc = iota((trows, fl_n), 0), iota((trows, fl_n), 1)
    tfl = tr // 8 * K + tr % K
    old = jnp.concatenate([old_ref[f, 0] for f in range(3)], axis=0)
    old_rows = sum(
        dot(onehot((tfl == tc) & (tr // 4 % 2 == c)), old[:, c * nr : (c + 1) * nr]) for c in range(2)
    )

    def mid_row(i):
        i = i + first_mid
        fl = i // 8 * K + i % K
        return fl // lev_n, fl % lev_n, i // 4 % 2

    levels = nlev * lev_n

    def mode_of(i, h):
        return lev_n * ((lev + h) % nlev) + i // 2

    i1, o1 = iota((2 * half, levels), 0), iota((2 * half, levels), 1)
    pick_out = onehot((o1 == mode_of(i1 % half, i1 // half)) & (i1 % half < 2 * lev_n), F32)
    field, level, cc = mid_row(iota((levels, mid), 1))
    pick_in = onehot(iota((levels, mid), 0) == lev_n * lev + level, F32)
    field, level, cc = mid_row(iota((2 * half, mid), 1))
    same_c = iota((2 * half, mid), 0) % 2 == cc
    m_in = mi_ref[...]
    w_div = jnp.where(same_c & (field == 1), fdot(fdot(pick_out, m_in), pick_in), 0.0)
    w_heat = jnp.where(same_c & (field == 2), fdot(fdot(pick_out, fdot(m_in, g_ref[...])), pick_in), 0.0)
    w1 = jnp.concatenate([w_div, w_heat], axis=0)
    im, om = iota((half, levels), 0), iota((half, levels), 1)
    own_mode = (om == lev_n * lev + im // 2) & (im < 2 * lev_n)
    rates = jnp.sum(jnp.where(own_mode, rates_ref[...][None, :], 0.0), axis=1, keepdims=True)
    i2, l2 = iota((2 * mid, levels), 0), iota((2 * mid, levels), 1)
    field, level, cc = mid_row(i2 % mid)
    pick_lev = onehot(l2 == lev_n * ((lev + i2 // mid) % nlev) + level, F32)
    im, om = iota((levels, half), 1), iota((levels, half), 0)
    pick_mode = onehot((om == lev_n * lev + im // 2) & (im < 2 * lev_n), F32)
    field, level, cc = mid_row(iota((2 * mid, half), 0) % mid)
    same_c = iota((2 * mid, half), 1) % 2 == cc
    w2 = jnp.where(same_c & (field == 1), fdot(fdot(pick_lev, mo_ref[...]), pick_mode), 0.0)
    w2 = w2 + jnp.where(same_c & (field == 2), -2.0 * fdot(fdot(pick_lev, mh_ref[...]), pick_mode), 0.0)
    field, level, cc = mid_row(iota((mid, 1), 0))
    stays = onehot(field != 1, F32)

    loads[10].wait()

    def wait1(i, carry):
        frm = lax.rem(me + n - i, n)
        pltpu.make_async_remote_copy(
            src_ref=send1.at[frm], dst_ref=recv1.at[frm], send_sem=s1.at[frm], recv_sem=r1.at[frm],
            device_id=(frm, lev), device_id_type=MESH,
        ).wait_recv()
        return carry

    lax.fori_loop(1, n, wait1, 0)

    cols = jnp.concatenate(
        [
            jnp.concatenate([recv1[d, :, g * jl : (g + 1) * jl] for d in range(n)], axis=1)
            for g in range(groups)
        ],
        axis=0,
    )
    both = lax.dot_general(cols, leg[...], NT, preferred_element_type=F32).reshape(groups, 2, 8, nr)
    total = jnp.where(iota((groups, 8, nr), 2) < first_pad, both[:, 0], both[:, 1])
    total = old_rows + jnp.where(used, total.reshape(trows, nr), 0.0)

    def exchange(src, dst, k):
        return pltpu.make_async_remote_copy(
            src_ref=src, dst_ref=dst, send_sem=es.at[k], recv_sem=er.at[k],
            device_id=(me, other), device_id_type=MESH,
        )

    tmid = total[first_mid:]
    w1s, t1s = split3(w1, tmid)
    res = dot(w1s, t1s)
    proj = res[: 2 * half] + 2.0 * lam * res[2 * half :]
    es1[...] = proj[half:].astype(BF16)
    exchange(es1, er1, 0).start()
    exchange(es1, er1, 0).wait()
    modal = (proj[:half] + er1[...].astype(F32)) / (1.0 + 4.0 * lam * rates)
    w2s, m2s = split3(w2, modal)
    res = dot(w2s, m2s)
    es2[...] = res[mid:].astype(BF16)
    exchange(es2, er2, 1).start()
    exchange(es2, er2, 1).wait()
    new_mid = tmid * stays + res[:mid] + er2[...].astype(F32)
    new = jnp.concatenate([total[:first_mid], new_mid], axis=0) if first_mid else new_mid
    new = jnp.where(used, new, 0.0)
    sides = jnp.stack(
        [
            jnp.where(first, new, 0.0).reshape(groups, 8, nr),
            jnp.where(first, 0.0, new).reshape(groups, 8, nr),
        ],
        axis=1,
    ).reshape(rows, nr).astype(BF16)
    grid = dot(sides, leg[...]).astype(BF16)
    for d in range(n):
        parts = [grid[g * 16 : (g + 1) * 16, d * jl : (d + 1) * jl] for g in range(groups)]
        if lanes > groups * jl:
            parts.append(jnp.zeros((16, lanes - groups * jl), BF16))
        send2[d] = jnp.concatenate(parts, axis=1)

    def copy2(i):
        to = lax.rem(me + i, n)
        return pltpu.make_async_remote_copy(
            src_ref=send2.at[to], dst_ref=recv2.at[me], send_sem=s2.at[to], recv_sem=r2.at[me],
            device_id=(to, lev), device_id_type=MESH,
        )

    def start2(i, carry):
        copy2(i).start()
        return carry

    lax.fori_loop(1, n, start2, 0)
    recv2[me] = send2[me]

    new_b = new.astype(BF16)
    sr, sc = iota((fl_n, trows), 0), iota((fl_n, trows), 1)
    sfl = sc // 8 * K + sc % K
    for c in range(2):
        part = dot(onehot((sfl == sr) & (sc // 4 % 2 == c)), new_b).astype(BF16)
        for f in range(3):
            spec_ref[f, 0, :, c * nr : (c + 1) * nr] = part[f * lev_n : (f + 1) * lev_n]

    spec_copy = pltpu.make_async_copy(spec_ref, spec_hbm, out_sem.at[0])
    spec_copy.start()

    def wait2(i, carry):
        copy1(i).wait_send()
        copy2(i).wait_send()
        frm = lax.rem(me + n - i, n)
        pltpu.make_async_remote_copy(
            src_ref=send2.at[frm], dst_ref=recv2.at[frm], send_sem=s2.at[frm], recv_sem=r2.at[frm],
            device_id=(frm, lev), device_id_type=MESH,
        ).wait_recv()
        return carry

    lax.fori_loop(1, n, wait2, 0)
    out_copies = []
    perm_back = onehot(pr == pc % K * q_n + pc // K)
    back = dot(perm_back, recv2[...].reshape(K * q_n, lanes))
    for g in range(groups):
        for k in range(K):
            fl = g * K + k
            if fl < fl_n:
                piece = back[k * q_n : (k + 1) * q_n, g * jl : (g + 1) * jl] * keep
                out_ref[fl // lev_n, fl % lev_n] = piece.astype(BF16)
                if fl % lev_n == lev_n - 1:
                    f = fl // lev_n
                    out_copies.append(pltpu.make_async_copy(out_ref.at[f], out_hbm.at[f], out_sem.at[1 + f]))
                    out_copies[-1].start()
    spec_copy.wait()
    for out_copy in out_copies:
        out_copy.wait()


def body(
    fourier_in, spectral_old, legendre, g_matrix, modes_in, modes_out, mode_heating, mode_rates, pair_ids, lat_ids,
    limits,
):
    n, nlev = lax.axis_size("wave"), lax.axis_size("lev")
    fields, lev_n, jl, q_n = fourier_in.shape
    groups = (fields * lev_n + K - 1) // K
    lanes = (groups * jl + 127) // 128 * 128
    nr, nlat = legendre.shape[1:]
    half = (2 * lev_n + 15) // 16 * 16
    mid = groups * 8 - lev_n // K * 8
    hbm = pl.BlockSpec(memory_space=pltpu.HBM)
    spec, out = pl.pallas_call(
        functools.partial(kernel, n, nlev),
        out_shape=(
            jax.ShapeDtypeStruct((fields, 1, lev_n, 2 * nr), BF16),
            jax.ShapeDtypeStruct((fields, lev_n, q_n, jl), BF16),
        ),
        in_specs=[hbm] * 11,
        out_specs=(hbm, hbm),
        scratch_shapes=[
            pltpu.VMEM((fields, 1, lev_n, 2 * nr), BF16),
            pltpu.VMEM((fields, lev_n, q_n, jl), BF16),
            pltpu.VMEM((fields, lev_n, q_n, jl), BF16),
            pltpu.VMEM((fields, 1, lev_n, 2 * nr), BF16),
            pltpu.VMEM((nr, nlat), BF16),
            pltpu.VMEM(g_matrix.shape, F32),
            pltpu.VMEM(g_matrix.shape, F32),
            pltpu.VMEM(g_matrix.shape, F32),
            pltpu.VMEM(g_matrix.shape, F32),
            pltpu.VMEM(mode_rates.shape, F32),
            pltpu.SMEM(pair_ids.shape, jnp.int32),
            pltpu.VMEM(lat_ids.shape, jnp.int32),
            pltpu.VMEM(limits.shape, jnp.int32),
            pltpu.VMEM((n, 16, lanes), BF16),
            pltpu.VMEM((n, 16, lanes), BF16),
            pltpu.VMEM((n, 16, lanes), BF16),
            pltpu.VMEM((n, 16, lanes), BF16),
            pltpu.VMEM((half, nr), BF16),
            pltpu.VMEM((half, nr), BF16),
            pltpu.VMEM((mid, nr), BF16),
            pltpu.VMEM((mid, nr), BF16),
            pltpu.SemaphoreType.DMA((1 + fields,)),
            pltpu.SemaphoreType.DMA((11,)),
            pltpu.SemaphoreType.DMA((n,)),
            pltpu.SemaphoreType.DMA((n,)),
            pltpu.SemaphoreType.DMA((n,)),
            pltpu.SemaphoreType.DMA((n,)),
            pltpu.SemaphoreType.DMA((2,)),
            pltpu.SemaphoreType.DMA((2,)),
        ],
        compiler_params=pltpu.CompilerParams(
            collective_id=0, has_side_effects=True, vmem_limit_bytes=63 * 1024 * 1024
        ),
        cost_estimate=pl.CostEstimate(flops=10**9, bytes_accessed=8 * 10**6, transcendentals=0),
    )(
        jnp.transpose(fourier_in, (0, 1, 3, 2)),
        jnp.transpose(spectral_old, (0, 2, 1, 3)),
        legendre,
        g_matrix,
        modes_in,
        modes_out,
        mode_heating,
        mode_rates,
        pair_ids,
        lat_ids,
        limits,
    )
    return jnp.transpose(spec, (0, 2, 1, 3)), jnp.transpose(out, (0, 1, 3, 2))


def solution(mesh):
    wave = P(None, "lev", "wave", None)
    return jax.shard_map(
        body,
        mesh=mesh,
        in_specs=(wave, wave, P("wave", None, None)) + (P(),) * 8,
        out_specs=(wave, wave),
        check_vma=False,
    )
```

profile of v0, /device:TPU:28, one launch (start us, length us, event | category | flops | bytes accessed | tf_op | source)
XLA Modules:
  0.0 38.7 jit_solution(11104258362064965793)
XLA Ops:
  0.6 34.4 %shard_map.122 = (bf16[3,1,14,2816]{3,2,1,0:T(8,128)(2,1)}, bf16[3,14,64,80]{3,2,1,0:T(8,128)(2,1)}) custom-call(bf16[3,14,64,80]{3,2,1,0:T(8,128)(2,1)} %bitcast.6, bf16[3,1,14,2816]{3,2,1,0:T(8,128)(2,1)} %bitcast.8, bf16[1,1408,1280]{2,1,0:T(8,128)(2,1)} %leg_hbm.1, f32[28,28]{1,0:T(8,128)} %g_hbm.1, f32[28,28]{1,0:T(8,128)} %mi_hbm.1, f32[28,28]{1,0:T(8,128)} %mo_hbm.1, ...), custom_call_target="tpu_custom_call" | custom-call | flops 1000000000 | bytes 8000000 | tf_op jit(solution)/shard_map/pallas_call | solution.py:307
  35.0 1.7 %copy.16 = bf16[3,14,1,2816]{3,1,2,0:T(8,128)(2,1)} copy(bf16[3,14,1,2816]{3,1,2,0:T(8,128)(2,1)} %bitcast.9) | data formatting | bytes 473088
  36.7 2.0 %copy.17 = bf16[3,14,80,64]{2,3,1,0:T(8,128)(2,1)} copy(bf16[3,14,80,64]{2,3,1,0:T(8,128)(2,1)} %bitcast.7) | data formatting | bytes 860160
where the time goes:
time: 38.9 us; the launch traced here: 38.7 us
  Pallas kernels  34.4 us (88%)
  local copies, waits for them, and re-layouts  3.67 us (9%)
  between operations  0.64 us (2%)
    pallas_call x1, Pallas kernels, body(): pl.pallas_call(functools.partial(kernel, n, nlev), out_shape=(jax.ShapeDt...  34.4 us
    unnamed x2, local copies, waits for them, and re-layouts  3.67 us

commit v1 on v0

v1 whole, which is shorter than its diff:
```python
import functools

import jax
import jax.numpy as jnp
from jax import lax
from jax.experimental import pallas as pl
from jax.experimental.pallas import tpu as pltpu
from jax.sharding import PartitionSpec as P

MMAX = 1280
BLOCK = 64
K = 8
CHUNK = 16
F32, BF16 = jnp.float32, jnp.bfloat16
MESH = pl.DeviceIdType.MESH
HI = lax.Precision.HIGHEST
NT = (((1,), (1,)), ((), ()))


def iota(shape, dim):
    return lax.broadcasted_iota(jnp.int32, shape, dim)


def dot(a, b):
    return jnp.dot(a, b, preferred_element_type=F32)


def fdot(a, b):
    return jnp.dot(a, b, precision=HI, preferred_element_type=F32)


def onehot(mask, dtype=BF16):
    return jnp.where(mask, 1.0, 0.0).astype(dtype)


def split3(left, right):
    lh = left.astype(BF16)
    ll = (left - lh.astype(F32)).astype(BF16)
    rh = right.astype(BF16)
    rl = (right - rh.astype(F32)).astype(BF16)
    return jnp.concatenate([lh, lh, ll], axis=1), jnp.concatenate([rh, rl, rh], axis=0)


def make_slots(lev_n):
    fill = -2 * lev_n % K
    slots = []
    for c in range(2):
        slots += [(f, l, c) for f in (1, 2) for l in range(lev_n)] + [(0, l, c) for l in range(fill)]
    rest = list(range(fill, lev_n))
    whole = len(rest) // K * K
    for c in range(2):
        slots += [(0, l, c) for l in rest[:whole]]
    for c in range(2):
        slots += [(0, l, c) for l in rest[whole:]]
    return [slots[i : i + K] for i in range(0, len(slots), K)]


def make_pieces(lev_n, jl):
    groups = make_slots(lev_n)
    td = (2 * lev_n + K - 1) // K
    ends = [td, 2 * td, len(groups)]
    lanes = (len(groups) * jl + 127) // 128 * 128
    up = [min((e * jl + 127) // 128 * 128, lanes) for e in ends]
    down = [e * jl // 128 * 128 for e in ends[:2]] + [lanes]
    return groups, [0] + ends, lanes, [0] + up, [0] + down


def kernel(
    n, nlev, x_hbm, old_hbm, leg_hbm, g_hbm, mi_hbm, mo_hbm, mh_hbm, rates_hbm, pid_hbm, lat_hbm, lim_hbm,
    spec_hbm, recv2,
    spec_ref, x_ref, old_ref, leg, g_ref, mi_ref, mo_ref, mh_ref, rates_ref, pid_ref, lat_ref, lim_ref,
    send1, recv1, send2, es, er, hot,
    out_sem, in_sem, s1, r1, s2, r2, es_sem, er_sem,
):
    lev_n = x_ref.shape[1]
    jl = x_ref.shape[3]
    groups, ends, lanes, up, down = make_pieces(lev_n, jl)
    nr, nlat = leg_hbm.shape[1:]
    me, lev = lax.axis_index("wave"), lax.axis_index("lev")
    other = lax.rem(lev + 1, nlev)
    plane = n // 4
    z, xy = me // plane, lax.rem(me, plane)
    low = z < 2

    def target(i):
        zi, k = i // plane, lax.rem(i, plane)
        far = jnp.where(low, 3 - zi, zi)
        near = jnp.where(zi == 2, z + 1 - 2 * lax.rem(z, 2), z)
        tz = jnp.where(zi < 2, far, near)
        return tz * plane + lax.rem(xy + k + zi // 3, plane)

    barrier = pltpu.get_barrier_semaphore()

    def greet(i, carry):
        pl.semaphore_signal(barrier, inc=1, device_id=(target(i), lev), device_id_type=MESH)
        return carry

    lax.fori_loop(0, n - 1, greet, 0)
    pl.semaphore_signal(barrier, inc=1, device_id=(me, other), device_id_type=MESH)

    pairs = [(x_hbm.at[f], x_ref.at[f]) for f in (1, 2, 0)] + [
        (pid_hbm, pid_ref), (lat_hbm, lat_ref), (lim_hbm, lim_ref), (g_hbm, g_ref), (mi_hbm, mi_ref),
        (mo_hbm, mo_ref), (mh_hbm, mh_ref), (rates_hbm, rates_ref), (old_hbm, old_ref), (leg_hbm.at[0], leg),
    ]
    loads = [pltpu.make_async_copy(src, dst, in_sem.at[i]) for i, (src, dst) in enumerate(pairs)]
    for load in loads:
        load.start()
    for load in loads[:3]:
        load.wait()

    pr, pc = iota((CHUNK * 16, 4 * CHUNK * K), 0), iota((CHUNK * 16, 4 * CHUNK * K), 1)
    base = pr % K * (4 * CHUNK) + pr // 16 * 4 + pr // 8 % 2 * 2

    def packed(g, h):
        slots = groups[g]
        part = jnp.zeros(pr.shape, jnp.int32)
        for k, (f, l, c) in enumerate(slots):
            if c:
                part = jnp.where(pr % K == k, 1, part)
        perm = onehot(pc == base + part)
        blocks = [x_ref[f, l, h * 4 * CHUNK : (h + 1) * 4 * CHUNK] for f, l, c in slots]
        blocks += [jnp.zeros_like(blocks[0])] * (K - len(slots))
        return perm, jnp.concatenate(blocks, axis=0)

    def pack_run(first, last, h):
        out, g = [], first
        while g < last:
            run = [g]
            parts = {c for f, l, c in groups[g]}
            while len(parts) == 1 and run[-1] + 1 < last and {c for f, l, c in groups[run[-1] + 1]} == parts and len(groups[run[-1] + 1]) == len(groups[g]):
                run.append(run[-1] + 1)
            perm = packed(g, h)[0]
            data = jnp.concatenate([packed(i, h)[1] for i in run], axis=1) if len(run) > 1 else packed(g, h)[1]
            out.append(dot(perm, data).astype(BF16))
            g = run[-1] + 1
        return out

    def copy1(p, to):
        at = pl.ds(up[p], up[p + 1] - up[p])
        return pltpu.make_async_remote_copy(
            src_ref=send1.at[to, :, at], dst_ref=recv1.at[me, :, at], send_sem=s1.at[p], recv_sem=r1.at[p],
            device_id=(to, lev), device_id_type=MESH,
        )

    def copy2(p, to):
        at = pl.ds(down[p], down[p + 1] - down[p])
        return pltpu.make_async_remote_copy(
            src_ref=send2.at[to, :, at], dst_ref=recv2.at[me, :, at], send_sem=s2.at[p], recv_sem=r2.at[p],
            device_id=(to, lev), device_id_type=MESH,
        )

    def start_all(copy, p):
        def start(i, carry):
            copy(p, target(i)).start()
            return carry

        lax.fori_loop(0, n - 1, start, 0)

    def whole(src, dst, bounds, ss, rr, p):
        at = pl.ds(bounds[p], bounds[p + 1] - bounds[p])
        return pltpu.make_async_remote_copy(
            src_ref=src.at[pl.ds(0, n - 1), :, at], dst_ref=dst.at[pl.ds(0, n - 1), :, at], send_sem=ss.at[p],
            recv_sem=rr.at[p], device_id=(me, other), device_id_type=MESH,
        )

    kept = [None] * (n // CHUNK)
    done = 0
    for p in range(3):
        lo, hi = up[p], up[p + 1]
        if hi > lo:
            last = min(len(groups), (hi + jl - 1) // jl)
            for h in range(n // CHUNK):
                rows = [] if kept[h] is None else [kept[h]]
                rows += pack_run(done, last, h)
                row = jnp.concatenate(rows, axis=1) if len(rows) > 1 else rows[0]
                if row.shape[1] < hi - lo:
                    row = jnp.concatenate([row, jnp.zeros((row.shape[0], hi - lo - row.shape[1]), BF16)], axis=1)
                send1[h * CHUNK : (h + 1) * CHUNK, :, lo:hi] = row[:, : hi - lo].reshape(CHUNK, 16, hi - lo)
                kept[h] = row[:, hi - lo :] if row.shape[1] > hi - lo else None
            done = last
            if p == 0:
                pl.semaphore_wait(barrier, n)
            start_all(copy1, p)
            recv1[me, :, lo:hi] = send1[me, :, lo:hi]

    for load in loads[3:12]:
        load.wait()

    hr = iota((16, nlat), 0)
    lim = lim_ref[...][None, :]
    lim_rows = jnp.where(hr == 0, lim // 8, jnp.where(hr == 1, lim % 8, 0)).astype(F32).astype(BF16)
    hot[...] = onehot(iota((nlat, nlat), 0) == lat_ref[...][None, :])
    got = dot(lim_rows, hot[...])
    row_limit = got[0:1] * 8.0 + got[1:2]
    a = pid_ref[me]
    wave = jnp.where(hr < 8, a, MMAX - 1 - a).astype(F32)
    keep = onehot(wave < row_limit, F32)
    keep_b = keep.astype(BF16)

    r = iota((1, nr), 1)
    first_pad = (MMAX - a + BLOCK - 1) // BLOCK * BLOCK
    first = r < first_pad
    used = (first & (r < MMAX - a)) | ((r >= first_pad) & (r - first_pad <= a))
    degree = jnp.where(first, a + r, MMAX - 1 - a + r - first_pad).astype(F32)
    lam = degree * (degree + 1.0) / float(MMAX * (MMAX - 1))

    levels = nlev * lev_n
    half = (levels + 15) // 16 * 16
    td = ends[1] * K
    mode = onehot(iota((half, levels), 0) == iota((half, levels), 1), F32)
    mode_t = onehot(iota((levels, half), 0) == iota((levels, half), 1), F32)
    own = lev_n * lev
    li, si = iota((levels, td), 0), iota((levels, td), 1)
    pick_div = onehot((li == own + si) & (si < lev_n), F32)
    pick_heat = onehot((li == own + si - lev_n) & (si >= lev_n) & (si < 2 * lev_n), F32)
    si, li = iota((td, levels), 0), iota((td, levels), 1)
    pick_div_t = onehot((li == own + si) & (si < lev_n), F32)
    pick_heat_t = onehot((li == own + si - lev_n) & (si >= lev_n) & (si < 2 * lev_n), F32)
    m_in = mi_ref[...]
    w1 = jnp.concatenate(
        [fdot(fdot(mode, m_in), pick_div), fdot(fdot(mode, fdot(m_in, g_ref[...])), pick_heat)], axis=0
    )
    w2 = fdot(fdot(pick_div_t, mo_ref[...]), mode_t) - 2.0 * fdot(fdot(pick_heat_t, mh_ref[...]), mode_t)
    rates = jnp.sum(
        jnp.where(iota((half, levels), 0) == iota((half, levels), 1), rates_ref[...][None, :], 0.0),
        axis=1, keepdims=True,
    )
    si = iota((td, 1), 0)
    stays = onehot(si >= lev_n, F32)

    def old_rows(p):
        slots = [s for g in groups[ends[p] : ends[p + 1]] for s in g]
        rows = (ends[p + 1] - ends[p]) * K
        total = None
        for c in range(2):
            if not any(s[2] == c for s in slots):
                continue
            row, col = iota((rows, 3 * lev_n), 0), iota((rows, 3 * lev_n), 1)
            src = jnp.full(row.shape, -1, jnp.int32)
            start = 0
            while start < len(slots):
                f, l, cc = slots[start]
                stop = start
                while stop < len(slots) and slots[stop] == (f, l + stop - start, cc):
                    stop += 1
                if cc == c:
                    src = jnp.where((row >= start) & (row < stop), row - start + f * lev_n + l, src)
                start = stop
            part = dot(onehot(col == src), old_all[:, c * nr : (c + 1) * nr])
            total = part if total is None else total + part
        return total

    old_all = jnp.concatenate([old_ref[f, 0] for f in range(3)], axis=0)
    olds = [old_rows(p) for p in range(3)]
    loads[12].wait()

    def forward(p):
        g_n = ends[p + 1] - ends[p]
        cols = jnp.concatenate(
            [
                jnp.concatenate([recv1[d, :, g * jl : (g + 1) * jl] for d in range(n)], axis=1) * keep_b
                for g in range(ends[p], ends[p + 1])
            ],
            axis=0,
        )
        both = lax.dot_general(cols, leg[...], NT, preferred_element_type=F32).reshape(g_n, 2, K, nr)
        total = jnp.where(iota((g_n, K, nr), 2) < first_pad, both[:, 0], both[:, 1]).reshape(g_n * K, nr)
        return jnp.where(used, olds[p] + total, 0.0)

    def inverse(p, new):
        g_n = ends[p + 1] - ends[p]
        sides = jnp.stack(
            [
                jnp.where(first, new, 0.0).reshape(g_n, K, nr),
                jnp.where(first, 0.0, new).reshape(g_n, K, nr),
            ],
            axis=1,
        ).reshape(g_n * 16, nr).astype(BF16)
        out = dot(sides, leg[...])
        return [(out[i * 16 : (i + 1) * 16] * keep).astype(BF16) for i in range(g_n)]

    def exchange(p):
        return pltpu.make_async_remote_copy(
            src_ref=es.at[p], dst_ref=er.at[p], send_sem=es_sem.at[p], recv_sem=er_sem.at[p],
            device_id=(me, other), device_id_type=MESH,
        )

    grids = []

    def send_piece(p):
        lo, hi = down[p], down[p + 1]
        if hi == lo:
            return
        for d in range(n):
            parts, at = [], lo
            while at < hi:
                g = at // jl
                if g >= len(grids):
                    parts.append(jnp.zeros((16, hi - at), BF16))
                    break
                stop = min(hi, (g + 1) * jl)
                parts.append(grids[g][:, d * jl + at - g * jl : d * jl + stop - g * jl])
                at = stop
            send2[d, :, lo:hi] = jnp.concatenate(parts, axis=1) if len(parts) > 1 else parts[0]
        start_all(copy2, p)

    news = []
    for p in range(3):
        if up[p + 1] > up[p]:
            whole(send1, recv1, up, s1, r1, p).wait_recv()
        total = forward(p)
        if p < 2:
            w1s, ts = split3(w1, total)
            res = dot(w1s, ts)
            proj = res[:half] + 2.0 * lam * res[half:]
            es[p] = proj.astype(BF16)
            exchange(p).start()
            exchange(p).wait()
            modal = (proj + er[p].astype(F32)) / (1.0 + 4.0 * lam * rates)
            w2s, ms = split3(w2, modal)
            total = jnp.where(used, total * stays + dot(w2s, ms), 0.0)
        grids += inverse(p, total)
        news.append(total)
        send_piece(p)

    own_copy = pltpu.make_async_copy(send2.at[me], recv2.at[me], out_sem.at[0])
    own_copy.start()

    flat = [s for g in groups for s in g]
    starts = [e * K for e in ends]

    def row_of(slot):
        i = flat.index(slot)
        p = max(j for j in range(3) if starts[j] <= i)
        return p, i - starts[p]

    for c in range(2):
        for f in range(3):
            parts, l = [], 0
            while l < lev_n:
                p, i = row_of((f, l, c))
                stop = l
                while stop < lev_n and row_of((f, stop, c)) == (p, i + stop - l):
                    stop += 1
                parts.append(news[p][i : i + stop - l])
                l = stop
            rows = jnp.concatenate(parts, axis=0) if len(parts) > 1 else parts[0]
            spec_ref[f, 0, :, c * nr : (c + 1) * nr] = rows.astype(BF16)
    spec_copy = pltpu.make_async_copy(spec_ref, spec_hbm, out_sem.at[1])
    spec_copy.start()

    for p in range(3):
        if up[p + 1] > up[p]:
            whole(send1, recv1, up, s1, r1, p).wait_send()
        if down[p + 1] > down[p]:
            whole(send2, recv2, down, s2, r2, p).wait_send()
    own_copy.wait()
    spec_copy.wait()
    for p in range(3):
        if down[p + 1] > down[p]:
            whole(send2, recv2, down, s2, r2, p).wait_recv()


def finish(n, lev_n, jl, got_hbm, spec_in, spec_hbm, out_hbm, got, out_ref, got_sem, sem):
    groups, ends, lanes, up, down = make_pieces(lev_n, jl)
    spec_copy = pltpu.make_async_copy(spec_in, spec_hbm, sem.at[3])
    load = pltpu.make_async_copy(got_hbm, got, got_sem)
    load.start()
    spec_copy.start()
    load.wait()
    where = {s: (g, k) for g, slots in enumerate(groups) for k, s in enumerate(slots)}
    pr, pc = iota((4 * CHUNK * K, 2 * CHUNK * 16), 0), iota((4 * CHUNK * K, 2 * CHUNK * 16), 1)
    q = pr % (4 * CHUNK)
    perm = onehot(pc == q % 2 * (CHUNK * 16) + q // 4 * 16 + q // 2 % 2 * 8 + pr // (4 * CHUNK))
    paired, single = [], {}
    for g, slots in enumerate(groups):
        partners = {where[(f, l, 1)] for f, l, c in slots if c == 0}
        if all(c == 0 for f, l, c in slots) and len({b for b, k in partners}) == 1:
            b = next(iter(partners))[0]
            if all(where[(f, l, 1)] == (b, k) for k, (f, l, c) in enumerate(slots)):
                paired.append((g, b))
    covered = {g for pair in paired for g in pair}
    for g, slots in enumerate(groups):
        if g not in covered:
            single[g] = slots
    for h in range(n // CHUNK):
        rows = got[h * CHUNK : (h + 1) * CHUNK].reshape(CHUNK * 16, lanes)
        qs = slice(h * 4 * CHUNK, (h + 1) * 4 * CHUNK)
        tops = jnp.concatenate([rows[:, g * jl : (g + 1) * jl] for g, b in paired], axis=1)
        bots = jnp.concatenate([rows[:, b * jl : (b + 1) * jl] for g, b in paired], axis=1)
        back = dot(perm, jnp.concatenate([tops, bots], axis=0)).astype(BF16)
        for i, (g, b) in enumerate(paired):
            for k, (f, l, c) in enumerate(groups[g]):
                out_ref[f, l, qs] = back[k * 4 * CHUNK : (k + 1) * 4 * CHUNK, i * jl : (i + 1) * jl]
        for g, slots in single.items():
            zero = [(f, l) for f, l, c in slots if c == 0]
            count = len(zero)
            sr, sc = iota((4 * CHUNK * count, CHUNK * 16), 0), iota((4 * CHUNK * count, CHUNK * 16), 1)
            sq, sk = sr % (4 * CHUNK), sr // (4 * CHUNK)
            some = onehot(sc == sq // 4 * 16 + sq // 2 % 2 * 8 + sk + count * (sq % 2))
            back = dot(some, rows[:, g * jl : (g + 1) * jl]).astype(BF16)
            for k, (f, l) in enumerate(zero):
                out_ref[f, l, qs] = back[k * 4 * CHUNK : (k + 1) * 4 * CHUNK]
    copies = [pltpu.make_async_copy(out_ref.at[f], out_hbm.at[f], sem.at[f]) for f in range(3)]
    for copy in copies:
        copy.start()
    for copy in copies:
        copy.wait()
    spec_copy.wait()


def body(
    fourier_in, spectral_old, legendre, g_matrix, modes_in, modes_out, mode_heating, mode_rates, pair_ids, lat_ids,
    limits,
):
    n, nlev = lax.axis_size("wave"), lax.axis_size("lev")
    fields, lev_n, jl, q_n = fourier_in.shape
    groups, ends, lanes, up, down = make_pieces(lev_n, jl)
    nr, nlat = legendre.shape[1:]
    half = (nlev * lev_n + 15) // 16 * 16
    hbm = pl.BlockSpec(memory_space=pltpu.HBM)
    spec, got = pl.pallas_call(
        functools.partial(kernel, n, nlev),
        out_shape=(
            jax.ShapeDtypeStruct((fields, 1, lev_n, 2 * nr), BF16),
            jax.ShapeDtypeStruct((n, 16, lanes), BF16),
        ),
        in_specs=[hbm] * 11,
        out_specs=(hbm, hbm),
        scratch_shapes=[
            pltpu.VMEM((fields, 1, lev_n, 2 * nr), BF16),
            pltpu.VMEM((fields, lev_n, q_n, jl), BF16),
            pltpu.VMEM((fields, 1, lev_n, 2 * nr), BF16),
            pltpu.VMEM((nr, nlat), BF16),
            pltpu.VMEM(g_matrix.shape, F32),
            pltpu.VMEM(g_matrix.shape, F32),
            pltpu.VMEM(g_matrix.shape, F32),
            pltpu.VMEM(g_matrix.shape, F32),
            pltpu.VMEM(mode_rates.shape, F32),
            pltpu.SMEM(pair_ids.shape, jnp.int32),
            pltpu.VMEM(lat_ids.shape, jnp.int32),
            pltpu.VMEM(limits.shape, jnp.int32),
            pltpu.VMEM((n, 16, lanes), BF16),
            pltpu.VMEM((n, 16, lanes), BF16),
            pltpu.VMEM((n, 16, lanes), BF16),
            pltpu.VMEM((2, half, nr), BF16),
            pltpu.VMEM((2, half, nr), BF16),
            pltpu.VMEM((nlat, nlat), BF16),
            pltpu.SemaphoreType.DMA((2,)),
            pltpu.SemaphoreType.DMA((13,)),
            pltpu.SemaphoreType.DMA((3,)),
            pltpu.SemaphoreType.DMA((3,)),
            pltpu.SemaphoreType.DMA((3,)),
            pltpu.SemaphoreType.DMA((3,)),
            pltpu.SemaphoreType.DMA((2,)),
            pltpu.SemaphoreType.DMA((2,)),
        ],
        compiler_params=pltpu.CompilerParams(
            collective_id=0, has_side_effects=True, vmem_limit_bytes=48 * 1024 * 1024
        ),
        cost_estimate=pl.CostEstimate(flops=10**9, bytes_accessed=8 * 10**6, transcendentals=0),
    )(
        jnp.transpose(fourier_in, (0, 1, 3, 2)),
        jnp.transpose(spectral_old, (0, 2, 1, 3)),
        legendre,
        g_matrix,
        modes_in,
        modes_out,
        mode_heating,
        mode_rates,
        pair_ids,
        lat_ids,
        limits,
    )
    spec, out = pl.pallas_call(
        functools.partial(finish, n, lev_n, jl),
        out_shape=(
            jax.ShapeDtypeStruct((fields, 1, lev_n, 2 * nr), BF16),
            jax.ShapeDtypeStruct((fields, lev_n, q_n, jl), BF16),
        ),
        in_specs=[hbm] * 2,
        out_specs=(hbm, hbm),
        scratch_shapes=[
            pltpu.VMEM((n, 16, lanes), BF16),
            pltpu.VMEM((fields, lev_n, q_n, jl), BF16),
            pltpu.SemaphoreType.DMA,
            pltpu.SemaphoreType.DMA((4,)),
        ],
        compiler_params=pltpu.CompilerParams(vmem_limit_bytes=48 * 1024 * 1024),
        cost_estimate=pl.CostEstimate(flops=2 * 10**8, bytes_accessed=2 * 10**6, transcendentals=0),
    )(got, spec)
    return jnp.transpose(spec, (0, 2, 1, 3)), jnp.transpose(out, (0, 1, 3, 2))


def solution(mesh):
    wave = P(None, "lev", "wave", None)
    return jax.shard_map(
        body,
        mesh=mesh,
        in_specs=(wave, wave, P("wave", None, None)) + (P(),) * 8,
        out_specs=(wave, wave),
        check_vma=False,
    )
```

time: 38.9 us -> 44.9 us (1.15)
  the two profiles are of different devices: /device:TPU:28 before, /device:TPU:0 now
where the time goes in v1:
time: 44.9 us; the launch traced here: 44.2 us
  Pallas kernels  33.9 us (76%)
  local copies, waits for them, and re-layouts  9.63 us (21%)
  between operations  0.66 us (1%)
    pallas_call x1, Pallas kernels, body(): pl.pallas_call(functools.partial(kernel, n, nlev), out_shape=(jax.ShapeDt...  32 us
    unnamed x22, local copies, waits for them, and re-layouts  9.63 us
    pallas_call x1, Pallas kernels, body(): pl.pallas_call(functools.partial(finish, n, lev_n, jl), out_shape=(jax.Sh...  1.9 us

profile of v1, /device:TPU:0, one launch (start us, length us, event | category | flops | bytes accessed | tf_op | source)
XLA Modules:
  0.0 44.2 jit_solution(15842330994918508627)
XLA Ops:
  0.6 0.0 copy-start
  0.6 2.0 %copy-done = bf16[1,1408,1280]{2,1,0:T(8,128)(2,1)S(1)} copy-done((bf16[1,1408,1280]{2,1,0:T(8,128)(2,1)S(1)}, bf16[1,1408,1280]{2,1,0:T(8,128)(2,1)}, u32[]{:S(2)}) %copy-start) | copy-done | bytes 3604504
  2.7 0.0 copy-start.1
  2.7 1.1 %copy-done.1 = bf16[3,14,80,64]{2,3,1,0:T(8,128)(2,1)S(1)} copy-done((bf16[3,14,80,64]{2,3,1,0:T(8,128)(2,1)S(1)}, bf16[3,14,80,64]{2,3,1,0:T(8,128)(2,1)}, u32[]{:S(2)}) %copy-start.1) | copy-done | bytes 430104
  3.8 0.0 copy-start.2
  3.8 1.0 %copy-done.2 = bf16[3,14,1,2816]{3,1,2,0:T(8,128)(2,1)S(1)} copy-done((bf16[3,14,1,2816]{3,1,2,0:T(8,128)(2,1)S(1)}, bf16[3,14,1,2816]{3,1,2,0:T(8,128)(2,1)}, u32[]{:S(2)}) %copy-start.2) | copy-done | bytes 236568
  4.7 0.0 copy-start.3
  4.7 0.7 %copy-done.3 = f32[28,28]{1,0:T(8,128)S(1)} copy-done((f32[28,28]{1,0:T(8,128)S(1)}, f32[28,28]{1,0:T(8,128)}, u32[]{:S(2)}) %copy-start.3) | copy-done | bytes 3160
  5.4 0.0 copy-start.4
  5.4 0.7 %copy-done.4 = f32[28,28]{1,0:T(8,128)S(1)} copy-done((f32[28,28]{1,0:T(8,128)S(1)}, f32[28,28]{1,0:T(8,128)}, u32[]{:S(2)}) %copy-start.4) | copy-done | bytes 3160
  6.1 0.0 copy-start.5
  6.1 0.7 %copy-done.5 = f32[28,28]{1,0:T(8,128)S(1)} copy-done((f32[28,28]{1,0:T(8,128)S(1)}, f32[28,28]{1,0:T(8,128)}, u32[]{:S(2)}) %copy-start.5) | copy-done | bytes 3160
  6.9 0.0 copy-start.6
  6.9 0.7 %copy-done.6 = f32[28,28]{1,0:T(8,128)S(1)} copy-done((f32[28,28]{1,0:T(8,128)S(1)}, f32[28,28]{1,0:T(8,128)}, u32[]{:S(2)}) %copy-start.6) | copy-done | bytes 3160
  7.6 0.0 copy-start.7
  7.6 0.7 %copy-done.7 = s32[1280]{0:T(1024)S(1)} copy-done((s32[1280]{0:T(1024)S(1)}, s32[1280]{0:T(1024)}, u32[]{:S(2)}) %copy-start.7) | copy-done | bytes 5144
  8.3 0.0 copy-start.8
  8.3 0.7 %copy-done.8 = s32[1280]{0:T(1024)S(1)} copy-done((s32[1280]{0:T(1024)S(1)}, s32[1280]{0:T(1024)}, u32[]{:S(2)}) %copy-start.8) | copy-done | bytes 5144
  9.0 0.0 copy-start.9
  9.0 0.7 %copy-done.9 = f32[28]{0:T(128)S(1)} copy-done((f32[28]{0:T(128)S(1)}, f32[28]{0:T(128)}, u32[]{:S(2)}) %copy-start.9) | copy-done | bytes 136
  9.6 0.0 copy-start.10
  9.6 0.7 %copy-done.10 = s32[16]{0:T(128)S(1)} copy-done((s32[16]{0:T(128)S(1)}, s32[16]{0:T(128)}, u32[]{:S(2)}) %copy-start.10) | copy-done | bytes 88
  10.3 32.0 %shard_map.122 = (bf16[3,1,14,2816]{3,2,1,0:T(8,128)(2,1)S(1)}, bf16[16,16,896]{2,1,0:T(8,128)(2,1)S(1)}) custom-call(bf16[3,14,64,80]{3,2,1,0:T(8,128)(2,1)S(1)} %bitcast.6, bf16[3,1,14,2816]{3,2,1,0:T(8,128)(2,1)S(1)} %bitcast.7, bf16[1,1408,1280]{2,1,0:T(8,128)(2,1)S(1)} %copy-done, f32[28,28]{1,0:T(8,128)S(1)} %copy-done.3, f32[28,28]{1,0:T(8,128)S(1)} %copy-done.4, ...), custom_call_target="tpu_custom_call" | custom-call | flops 1000000000 | bytes 8000000 | tf_op jit(solution)/shard_map/pallas_call | solution.py:422
  42.3 1.9 %shard_map.123 = (bf16[3,1,14,2816]{3,2,1,0:T(8,128)(2,1)}, bf16[3,14,64,80]{3,2,1,0:T(8,128)(2,1)}) custom-call(bf16[16,16,896]{2,1,0:T(8,128)(2,1)S(1)} %get-tuple-element.6.got_hbm, bf16[3,1,14,2816]{3,2,1,0:T(8,128)(2,1)S(1)} %get-tuple-element.7.spec_in), custom_call_target="tpu_custom_call" | custom-call | flops 200000000 | bytes 2000000 | tf_op jit(solution)/shard_map/pallas_call | solution.py:475
Async XLA Ops:
  0.6 2.0 %copy-start = (bf16[1,1408,1280]{2,1,0:T(8,128)(2,1)S(1)}, bf16[1,1408,1280]{2,1,0:T(8,128)(2,1)}, u32[]{:S(2)}) copy-start(bf16[1,1408,1280]{2,1,0:T(8,128)(2,1)} %leg_hbm.1) | copy-start | bytes 10813444
  2.7 1.1 %copy-start.1 = (bf16[3,14,80,64]{2,3,1,0:T(8,128)(2,1)S(1)}, bf16[3,14,80,64]{2,3,1,0:T(8,128)(2,1)}, u32[]{:S(2)}) copy-start(bf16[3,14,80,64]{2,3,1,0:T(8,128)(2,1)} %param.11) | copy-start | bytes 1290244
  3.8 1.0 %copy-start.2 = (bf16[3,14,1,2816]{3,1,2,0:T(8,128)(2,1)S(1)}, bf16[3,14,1,2816]{3,1,2,0:T(8,128)(2,1)}, u32[]{:S(2)}) copy-start(bf16[3,14,1,2816]{3,1,2,0:T(8,128)(2,1)} %param.12) | copy-start | bytes 709636
  4.7 0.7 %copy-start.3 = (f32[28,28]{1,0:T(8,128)S(1)}, f32[28,28]{1,0:T(8,128)}, u32[]{:S(2)}) copy-start(f32[28,28]{1,0:T(8,128)} %g_hbm.1) | copy-start | bytes 9412
  5.4 0.7 %copy-start.4 = (f32[28,28]{1,0:T(8,128)S(1)}, f32[28,28]{1,0:T(8,128)}, u32[]{:S(2)}) copy-start(f32[28,28]{1,0:T(8,128)} %mi_hbm.1) | copy-start | bytes 9412
  6.1 0.7 %copy-start.5 = (f32[28,28]{1,0:T(8,128)S(1)}, f32[28,28]{1,0:T(8,128)}, u32[]{:S(2)}) copy-start(f32[28,28]{1,0:T(8,128)} %mo_hbm.1) | copy-start | bytes 9412
  6.9 0.7 %copy-start.6 = (f32[28,28]{1,0:T(8,128)S(1)}, f32[28,28]{1,0:T(8,128)}, u32[]{:S(2)}) copy-start(f32[28,28]{1,0:T(8,128)} %mh_hbm.1) | copy-start | bytes 9412
  7.6 0.7 %copy-start.7 = (s32[1280]{0:T(1024)S(1)}, s32[1280]{0:T(1024)}, u32[]{:S(2)}) copy-start(s32[1280]{0:T(1024)} %lat_hbm.1) | copy-start | bytes 15364
  8.3 0.7 %copy-start.8 = (s32[1280]{0:T(1024)S(1)}, s32[1280]{0:T(1024)}, u32[]{:S(2)}) copy-start(s32[1280]{0:T(1024)} %lim_hbm.1) | copy-start | bytes 15364
  9.0 0.7 %copy-start.9 = (f32[28]{0:T(128)S(1)}, f32[28]{0:T(128)}, u32[]{:S(2)}) copy-start(f32[28]{0:T(128)} %rates_hbm.1) | copy-start | bytes 340
  9.6 0.7 %copy-start.10 = (s32[16]{0:T(128)S(1)}, s32[16]{0:T(128)}, u32[]{:S(2)}) copy-start(s32[16]{0:T(128)} %pid_hbm.1) | copy-start | bytes 196

commit v2 on v1

--- a/solution.py
+++ b/solution.py
@@ -460,17 +460,22 @@
         ),
         cost_estimate=pl.CostEstimate(flops=10**9, bytes_accessed=8 * 10**6, transcendentals=0),
     )(
-        jnp.transpose(fourier_in, (0, 1, 3, 2)),
-        jnp.transpose(spectral_old, (0, 2, 1, 3)),
-        legendre,
-        g_matrix,
-        modes_in,
-        modes_out,
-        mode_heating,
-        mode_rates,
-        pair_ids,
-        lat_ids,
-        limits,
+        *[
+            pltpu.with_memory_space_constraint(x, pltpu.HBM)
+            for x in (
+                jnp.transpose(fourier_in, (0, 1, 3, 2)),
+                jnp.transpose(spectral_old, (0, 2, 1, 3)),
+                legendre,
+                g_matrix,
+                modes_in,
+                modes_out,
+                mode_heating,
+                mode_rates,
+                pair_ids,
+                lat_ids,
+                limits,
+            )
+        ]
     )
     spec, out = pl.pallas_call(
         functools.partial(finish, n, lev_n, jl),

time: 44.9 us -> 34.8 us (0.78); the launches traced: 44.2 us -> 34.6 us
  local copies, waits for them, and re-layouts: 9.63 us -> 0 us
    unnamed x22 -> x0, local copies, waits for them, and re-layouts: 9.63 us -> none
where the time goes in v2:
time: 34.8 us; the launch traced here: 34.6 us
  Pallas kernels  34 us (98%)
  between operations  0.64 us (2%)
    pallas_call x1, Pallas kernels, body(): pl.pallas_call(functools.partial(kernel, n, nlev), out_shape=(jax.ShapeDt...  32.1 us
    pallas_call x1, Pallas kernels, body(): pl.pallas_call(functools.partial(finish, n, lev_n, jl), out_shape=(jax.Sh...  1.9 us

profile of v2, /device:TPU:0, one launch (start us, length us, event | category | flops | bytes accessed | tf_op | source)
XLA Modules:
  0.0 34.6 jit_solution(11587004352592448394)
XLA Ops:
  0.6 32.1 %shard_map.122 = (bf16[3,1,14,2816]{3,2,1,0:T(8,128)(2,1)S(1)}, bf16[16,16,896]{2,1,0:T(8,128)(2,1)S(1)}) custom-call(bf16[3,14,64,80]{3,2,1,0:T(8,128)(2,1)} %bitcast.6, bf16[3,1,14,2816]{3,2,1,0:T(8,128)(2,1)} %bitcast.7, bf16[1,1408,1280]{2,1,0:T(8,128)(2,1)} %leg_hbm.1, f32[28,28]{1,0:T(8,128)} %g_hbm.1, f32[28,28]{1,0:T(8,128)} %mi_hbm.1, ...), custom_call_target="tpu_custom_call" | custom-call | flops 1000000000 | bytes 8000000 | tf_op jit(solution)/shard_map/pallas_call | solution.py:422
  32.7 1.9 %shard_map.123 = (bf16[3,1,14,2816]{3,2,1,0:T(8,128)(2,1)}, bf16[3,14,64,80]{3,2,1,0:T(8,128)(2,1)}) custom-call(bf16[16,16,896]{2,1,0:T(8,128)(2,1)S(1)} %get-tuple-element.6.got_hbm, bf16[3,1,14,2816]{3,2,1,0:T(8,128)(2,1)S(1)} %get-tuple-element.7.spec_in), custom_call_target="tpu_custom_call" | custom-call | flops 200000000 | bytes 2000000 | tf_op jit(solution)/shard_map/pallas_call | solution.py:480

commit v3 on v2

--- a/solution.py
+++ b/solution.py
@@ -43,38 +43,59 @@
 
 def make_slots(lev_n):
     fill = -2 * lev_n % K
-    slots = []
-    for c in range(2):
-        slots += [(f, l, c) for f in (1, 2) for l in range(lev_n)] + [(0, l, c) for l in range(fill)]
     rest = list(range(fill, lev_n))
     whole = len(rest) // K * K
+    slots = []
+    for levels in (rest[:whole], rest[whole:]):
+        for c in range(2):
+            slots += [(0, l, c) for l in levels]
+    groups = [slots[i : i + K] for i in range(0, len(slots), K)]
+    ends = [0, len(groups)]
     for c in range(2):
-        slots += [(0, l, c) for l in rest[:whole]]
-    for c in range(2):
-        slots += [(0, l, c) for l in rest[whole:]]
-    return [slots[i : i + K] for i in range(0, len(slots), K)]
+        slots = [(f, l, c) for f in (1, 2) for l in range(lev_n)] + [(0, l, c) for l in range(fill)]
+        groups += [slots[i : i + K] for i in range(0, len(slots), K)]
+        ends.append(len(groups))
+    return groups, ends
 
 
 def make_pieces(lev_n, jl):
-    groups = make_slots(lev_n)
-    td = (2 * lev_n + K - 1) // K
-    ends = [td, 2 * td, len(groups)]
-    lanes = (len(groups) * jl + 127) // 128 * 128
-    up = [min((e * jl + 127) // 128 * 128, lanes) for e in ends]
-    down = [e * jl // 128 * 128 for e in ends[:2]] + [lanes]
-    return groups, [0] + ends, lanes, [0] + up, [0] + down
+    groups, ends = make_slots(lev_n)
+    count = len(groups)
+    lanes = (count * jl + 127) // 128 * 128
+    pad = -ends[1] * jl % 128
+    if count * jl + pad > lanes:
+        pad = 0
+    first = [g * jl + (pad if g >= ends[1] else 0) for g in range(count)] + [lanes]
+    stops = [first[ends[1]], first[ends[2]], lanes]
+    up = [min((e + 127) // 128 * 128, lanes) for e in stops]
+    down = [e // 128 * 128 for e in stops]
+    return groups, ends, lanes, first, [0] + up, [0] + down
+
+
+def lane_parts(first, jl, lo, hi):
+    parts, at = [], lo
+    while at < hi:
+        g = max(i for i in range(len(first) - 1) if first[i] <= at)
+        if at < first[g] + jl:
+            stop = min(hi, first[g] + jl)
+            parts.append((g, at - first[g], stop - first[g]))
+        else:
+            stop = min(hi, first[g + 1])
+            parts.append((None, 0, stop - at))
+        at = stop
+    return parts
 
 
 def kernel(
     n, nlev, x_hbm, old_hbm, leg_hbm, g_hbm, mi_hbm, mo_hbm, mh_hbm, rates_hbm, pid_hbm, lat_hbm, lim_hbm,
     spec_hbm, recv2,
     spec_ref, x_ref, old_ref, leg, g_ref, mi_ref, mo_ref, mh_ref, rates_ref, pid_ref, lat_ref, lim_ref,
-    send1, recv1, send2, es, er, hot,
+    send1, recv1, send2, es, er, hot, turned,
     out_sem, in_sem, s1, r1, s2, r2, es_sem, er_sem,
 ):
     lev_n = x_ref.shape[1]
     jl = x_ref.shape[3]
-    groups, ends, lanes, up, down = make_pieces(lev_n, jl)
+    groups, ends, lanes, base, up, down = make_pieces(lev_n, jl)
     nr, nlat = leg_hbm.shape[1:]
     me, lev = lax.axis_index("wave"), lax.axis_index("lev")
     other = lax.rem(lev + 1, nlev)
@@ -89,49 +110,57 @@
         tz = jnp.where(zi < 2, far, near)
         return tz * plane + lax.rem(xy + k + zi // 3, plane)
 
-    barrier = pltpu.get_barrier_semaphore()
-
-    def greet(i, carry):
-        pl.semaphore_signal(barrier, inc=1, device_id=(target(i), lev), device_id_type=MESH)
-        return carry
-
-    lax.fori_loop(0, n - 1, greet, 0)
-    pl.semaphore_signal(barrier, inc=1, device_id=(me, other), device_id_type=MESH)
-
-    pairs = [(x_hbm.at[f], x_ref.at[f]) for f in (1, 2, 0)] + [
+    pairs = [(x_hbm.at[f], x_ref.at[f]) for f in (0, 1, 2)] + [
         (pid_hbm, pid_ref), (lat_hbm, lat_ref), (lim_hbm, lim_ref), (g_hbm, g_ref), (mi_hbm, mi_ref),
         (mo_hbm, mo_ref), (mh_hbm, mh_ref), (rates_hbm, rates_ref), (old_hbm, old_ref), (leg_hbm.at[0], leg),
     ]
     loads = [pltpu.make_async_copy(src, dst, in_sem.at[i]) for i, (src, dst) in enumerate(pairs)]
-    for load in loads:
+    for load in loads[:3]:
         load.start()
-    for load in loads[:3]:
-        load.wait()
+    barrier = pltpu.get_barrier_semaphore()
+
+    def greet(i, carry):
+        pl.semaphore_signal(barrier, inc=1, device_id=(target(i), lev), device_id_type=MESH)
+        return carry
+
+    lax.fori_loop(0, n - 1, greet, 0)
+    pl.semaphore_signal(barrier, inc=1, device_id=(me, other), device_id_type=MESH)
+    for load in loads[3:]:
+        load.start()
 
     pr, pc = iota((CHUNK * 16, 4 * CHUNK * K), 0), iota((CHUNK * 16, 4 * CHUNK * K), 1)
-    base = pr % K * (4 * CHUNK) + pr // 16 * 4 + pr // 8 % 2 * 2
-
-    def packed(g, h):
-        slots = groups[g]
+    home = pr % K * (4 * CHUNK) + pr // 16 * 4 + pr // 8 % 2 * 2
+
+    def perm_of(g):
         part = jnp.zeros(pr.shape, jnp.int32)
-        for k, (f, l, c) in enumerate(slots):
+        for k, (f, l, c) in enumerate(groups[g]):
             if c:
                 part = jnp.where(pr % K == k, 1, part)
-        perm = onehot(pc == base + part)
-        blocks = [x_ref[f, l, h * 4 * CHUNK : (h + 1) * 4 * CHUNK] for f, l, c in slots]
-        blocks += [jnp.zeros_like(blocks[0])] * (K - len(slots))
-        return perm, jnp.concatenate(blocks, axis=0)
+        return onehot(pc == home + part)
+
+    def parts_of(g):
+        return tuple(c for f, l, c in groups[g])
+
+    perms = {}
+    for g in range(len(groups)):
+        if parts_of(g) not in perms:
+            perms[parts_of(g)] = perm_of(g)
+
+    def packed(g, h):
+        blocks = [x_ref[f, l, h * 4 * CHUNK : (h + 1) * 4 * CHUNK] for f, l, c in groups[g]]
+        blocks += [jnp.zeros_like(blocks[0])] * (K - len(blocks))
+        return jnp.concatenate(blocks, axis=0)
 
     def pack_run(first, last, h):
         out, g = [], first
         while g < last:
             run = [g]
-            parts = {c for f, l, c in groups[g]}
-            while len(parts) == 1 and run[-1] + 1 < last and {c for f, l, c in groups[run[-1] + 1]} == parts and len(groups[run[-1] + 1]) == len(groups[g]):
+            while run[-1] + 1 < last and parts_of(run[-1] + 1) == parts_of(g):
                 run.append(run[-1] + 1)
-            perm = packed(g, h)[0]
-            data = jnp.concatenate([packed(i, h)[1] for i in run], axis=1) if len(run) > 1 else packed(g, h)[1]
-            out.append(dot(perm, data).astype(BF16))
+            data = [packed(i, h) for i in run]
+            data = jnp.concatenate(data, axis=1) if len(run) > 1 else data[0]
+            data = dot(perms[parts_of(g)], data).astype(BF16)
+            out += [data[:, i * jl : (i + 1) * jl] for i in range(len(run))]
             g = run[-1] + 1
         return out
 
@@ -154,7 +183,11 @@
             copy(p, target(i)).start()
             return carry
 
-        lax.fori_loop(0, n - 1, start, 0)
+        def start_up(i, carry):
+            copy(p, jnp.where(i < me, i, i + 1)).start()
+            return carry
+
+        lax.fori_loop(0, n - 1, start_up if copy is copy2 else start, 0)
 
     def whole(src, dst, bounds, ss, rr, p):
         at = pl.ds(bounds[p], bounds[p + 1] - bounds[p])
@@ -163,25 +196,31 @@
             recv_sem=rr.at[p], device_id=(me, other), device_id_type=MESH,
         )
 
-    kept = [None] * (n // CHUNK)
     done = 0
+    held = {}
     for p in range(3):
         lo, hi = up[p], up[p + 1]
-        if hi > lo:
-            last = min(len(groups), (hi + jl - 1) // jl)
-            for h in range(n // CHUNK):
-                rows = [] if kept[h] is None else [kept[h]]
-                rows += pack_run(done, last, h)
-                row = jnp.concatenate(rows, axis=1) if len(rows) > 1 else rows[0]
-                if row.shape[1] < hi - lo:
-                    row = jnp.concatenate([row, jnp.zeros((row.shape[0], hi - lo - row.shape[1]), BF16)], axis=1)
-                send1[h * CHUNK : (h + 1) * CHUNK, :, lo:hi] = row[:, : hi - lo].reshape(CHUNK, 16, hi - lo)
-                kept[h] = row[:, hi - lo :] if row.shape[1] > hi - lo else None
-            done = last
-            if p == 0:
-                pl.semaphore_wait(barrier, n)
-            start_all(copy1, p)
-            recv1[me, :, lo:hi] = send1[me, :, lo:hi]
+        if p == 0:
+            loads[0].wait()
+        if p == 1:
+            loads[1].wait()
+            loads[2].wait()
+        if hi == lo:
+            continue
+        parts = lane_parts(base, jl, lo, hi)
+        last = max([g + 1 for g, u, v in parts if g is not None] + [done])
+        for h in range(n // CHUNK):
+            held.update({(h, done + i): x for i, x in enumerate(pack_run(done, last, h))})
+            row = [
+                jnp.zeros((CHUNK * 16, v), BF16) if g is None else held[h, g][:, u:v] for g, u, v in parts
+            ]
+            row = jnp.concatenate(row, axis=1) if len(row) > 1 else row[0]
+            send1[h * CHUNK : (h + 1) * CHUNK, :, lo:hi] = row.reshape(CHUNK, 16, hi - lo)
+        done = last
+        if p == 0:
+            pl.semaphore_wait(barrier, n)
+        start_all(copy1, p)
+        recv1[me, :, lo:hi] = send1[me, :, lo:hi]
 
     for load in loads[3:12]:
         load.wait()
@@ -206,7 +245,7 @@
 
     levels = nlev * lev_n
     half = (levels + 15) // 16 * 16
-    td = ends[1] * K
+    td = (ends[2] - ends[1]) * K
     mode = onehot(iota((half, levels), 0) == iota((half, levels), 1), F32)
     mode_t = onehot(iota((levels, half), 0) == iota((levels, half), 1), F32)
     own = lev_n * lev
@@ -254,16 +293,23 @@
     olds = [old_rows(p) for p in range(3)]
     loads[12].wait()
 
+    def turn(i, carry):
+        at = pl.ds(pl.multiple_of(i * 128, 128), 128)
+        turned[:, at] = leg[at, :].T
+        return carry
+
+    lax.fori_loop(0, nr // 128, turn, 0)
+
     def forward(p):
         g_n = ends[p + 1] - ends[p]
         cols = jnp.concatenate(
             [
-                jnp.concatenate([recv1[d, :, g * jl : (g + 1) * jl] for d in range(n)], axis=1) * keep_b
+                jnp.concatenate([recv1[d, :, base[g] : base[g] + jl] for d in range(n)], axis=1) * keep_b
                 for g in range(ends[p], ends[p + 1])
             ],
             axis=0,
         )
-        both = lax.dot_general(cols, leg[...], NT, preferred_element_type=F32).reshape(g_n, 2, K, nr)
+        both = dot(cols, turned[...]).reshape(g_n, 2, K, nr)
         total = jnp.where(iota((g_n, K, nr), 2) < first_pad, both[:, 0], both[:, 1]).reshape(g_n * K, nr)
         return jnp.where(used, olds[p] + total, 0.0)
 
@@ -287,46 +333,62 @@
 
     grids = []
 
+    def fill_piece(p):
+        lo, hi = down[p], down[p + 1]
+        for d in range(n if hi > lo else 0):
+            row = [
+                jnp.zeros((16, v), BF16) if g is None else grids[g][:, d * jl + u : d * jl + v]
+                for g, u, v in lane_parts(base, jl, lo, hi)
+            ]
+            send2[d, :, lo:hi] = jnp.concatenate(row, axis=1) if len(row) > 1 else row[0]
+
     def send_piece(p):
-        lo, hi = down[p], down[p + 1]
-        if hi == lo:
-            return
-        for d in range(n):
-            parts, at = [], lo
-            while at < hi:
-                g = at // jl
-                if g >= len(grids):
-                    parts.append(jnp.zeros((16, hi - at), BF16))
-                    break
-                stop = min(hi, (g + 1) * jl)
-                parts.append(grids[g][:, d * jl + at - g * jl : d * jl + stop - g * jl])
-                at = stop
-            send2[d, :, lo:hi] = jnp.concatenate(parts, axis=1) if len(parts) > 1 else parts[0]
-        start_all(copy2, p)
-
-    news = []
-    for p in range(3):
+        if down[p + 1] > down[p]:
+            start_all(copy2, p)
+
+    def arrive(p):
         if up[p + 1] > up[p]:
             whole(send1, recv1, up, s1, r1, p).wait_recv()
-        total = forward(p)
-        if p < 2:
-            w1s, ts = split3(w1, total)
-            res = dot(w1s, ts)
-            proj = res[:half] + 2.0 * lam * res[half:]
-            es[p] = proj.astype(BF16)
-            exchange(p).start()
-            exchange(p).wait()
-            modal = (proj + er[p].astype(F32)) / (1.0 + 4.0 * lam * rates)
-            w2s, ms = split3(w2, modal)
-            total = jnp.where(used, total * stays + dot(w2s, ms), 0.0)
-        grids += inverse(p, total)
-        news.append(total)
-        send_piece(p)
+
+    def project(p, total):
+        w1s, ts = split3(w1, total)
+        res = dot(w1s, ts)
+        proj = res[:half] + 2.0 * lam * res[half:]
+        es[p - 1] = proj.astype(BF16)
+        exchange(p - 1).start()
+        return proj
+
+    def step(p, total, proj):
+        exchange(p - 1).wait()
+        modal = (proj + er[p - 1].astype(F32)) / (1.0 + 4.0 * lam * rates)
+        w2s, ms = split3(w2, modal)
+        return jnp.where(used, total * stays + dot(w2s, ms), 0.0)
+
+    arrive(0)
+    vort = forward(0)
+    grids += inverse(0, vort)
+    fill_piece(0)
+    arrive(1)
+    total1 = forward(1)
+    proj1 = project(1, total1)
+    send_piece(0)
+    arrive(2)
+    total2 = forward(2)
+    proj2 = project(2, total2)
+    new1 = step(1, total1, proj1)
+    grids += inverse(1, new1)
+    fill_piece(1)
+    send_piece(1)
+    new2 = step(2, total2, proj2)
+    grids += inverse(2, new2)
+    fill_piece(2)
+    send_piece(2)
+    news = [vort, new1, new2]
 
     own_copy = pltpu.make_async_copy(send2.at[me], recv2.at[me], out_sem.at[0])
     own_copy.start()
 
-    flat = [s for g in groups for s in g]
+    flat = [s for g in groups for s in g + [None] * (K - len(g))]
     starts = [e * K for e in ends]
 
     def row_of(slot):
@@ -361,13 +423,10 @@
             whole(send2, recv2, down, s2, r2, p).wait_recv()
 
 
-def finish(n, lev_n, jl, got_hbm, spec_in, spec_hbm, out_hbm, got, out_ref, got_sem, sem):
-    groups, ends, lanes, up, down = make_pieces(lev_n, jl)
+def finish(n, lev_n, jl, got, spec_in, spec_hbm, out_hbm, out_ref, sem):
+    groups, ends, lanes, base, up, down = make_pieces(lev_n, jl)
     spec_copy = pltpu.make_async_copy(spec_in, spec_hbm, sem.at[3])
-    load = pltpu.make_async_copy(got_hbm, got, got_sem)
-    load.start()
     spec_copy.start()
-    load.wait()
     where = {s: (g, k) for g, slots in enumerate(groups) for k, s in enumerate(slots)}
     pr, pc = iota((4 * CHUNK * K, 2 * CHUNK * 16), 0), iota((4 * CHUNK * K, 2 * CHUNK * 16), 1)
     q = pr % (4 * CHUNK)
@@ -386,8 +445,8 @@
     for h in range(n // CHUNK):
         rows = got[h * CHUNK : (h + 1) * CHUNK].reshape(CHUNK * 16, lanes)
         qs = slice(h * 4 * CHUNK, (h + 1) * 4 * CHUNK)
-        tops = jnp.concatenate([rows[:, g * jl : (g + 1) * jl] for g, b in paired], axis=1)
-        bots = jnp.concatenate([rows[:, b * jl : (b + 1) * jl] for g, b in paired], axis=1)
+        tops = jnp.concatenate([rows[:, base[g] : base[g] + jl] for g, b in paired], axis=1)
+        bots = jnp.concatenate([rows[:, base[b] : base[b] + jl] for g, b in paired], axis=1)
         back = dot(perm, jnp.concatenate([tops, bots], axis=0)).astype(BF16)
         for i, (g, b) in enumerate(paired):
             for k, (f, l, c) in enumerate(groups[g]):
@@ -398,7 +457,7 @@
             sr, sc = iota((4 * CHUNK * count, CHUNK * 16), 0), iota((4 * CHUNK * count, CHUNK * 16), 1)
             sq, sk = sr % (4 * CHUNK), sr // (4 * CHUNK)
             some = onehot(sc == sq // 4 * 16 + sq // 2 % 2 * 8 + sk + count * (sq % 2))
-            back = dot(some, rows[:, g * jl : (g + 1) * jl]).astype(BF16)
+            back = dot(some, rows[:, base[g] : base[g] + jl]).astype(BF16)
             for k, (f, l) in enumerate(zero):
                 out_ref[f, l, qs] = back[k * 4 * CHUNK : (k + 1) * 4 * CHUNK]
     copies = [pltpu.make_async_copy(out_ref.at[f], out_hbm.at[f], sem.at[f]) for f in range(3)]
@@ -415,7 +474,7 @@
 ):
     n, nlev = lax.axis_size("wave"), lax.axis_size("lev")
     fields, lev_n, jl, q_n = fourier_in.shape
-    groups, ends, lanes, up, down = make_pieces(lev_n, jl)
+    groups, ends, lanes, base, up, down = make_pieces(lev_n, jl)
     nr, nlat = legendre.shape[1:]
     half = (nlev * lev_n + 15) // 16 * 16
     hbm = pl.BlockSpec(memory_space=pltpu.HBM)
@@ -446,6 +505,7 @@
             pltpu.VMEM((2, half, nr), BF16),
             pltpu.VMEM((2, half, nr), BF16),
             pltpu.VMEM((nlat, nlat), BF16),
+            pltpu.VMEM((nlat, nr), BF16),
             pltpu.SemaphoreType.DMA((2,)),
             pltpu.SemaphoreType.DMA((13,)),
             pltpu.SemaphoreType.DMA((3,)),
@@ -483,12 +543,10 @@
             jax.ShapeDtypeStruct((fields, 1, lev_n, 2 * nr), BF16),
             jax.ShapeDtypeStruct((fields, lev_n, q_n, jl), BF16),
         ),
-        in_specs=[hbm] * 2,
+        in_specs=[pl.BlockSpec(memory_space=pltpu.VMEM)] * 2,
         out_specs=(hbm, hbm),
         scratch_shapes=[
-            pltpu.VMEM((n, 16, lanes), BF16),
             pltpu.VMEM((fields, lev_n, q_n, jl), BF16),
-            pltpu.SemaphoreType.DMA,
             pltpu.SemaphoreType.DMA((4,)),
         ],
         compiler_params=pltpu.CompilerParams(vmem_limit_bytes=48 * 1024 * 1024),

time: 34.8 us -> 32.7 us (0.940)
  Pallas kernels: 34 us -> 32 us
    pallas_call x1, Pallas kernels: 32.1 us -> 30.3 us  [body(): pl.pallas_call(functools.partial(kernel, n, nlev), out_shape=(jax.ShapeDt...]
where the time goes in v3:
time: 32.7 us; the launch traced here: 32.6 us
  Pallas kernels  32 us (98%)
  between operations  0.64 us (2%)
    pallas_call x1, Pallas kernels, body(): pl.pallas_call(functools.partial(kernel, n, nlev), out_shape=(jax.ShapeDt...  30.3 us
    pallas_call x1, Pallas kernels, body(): pl.pallas_call(functools.partial(finish, n, lev_n, jl), out_shape=(jax.Sh...  1.68 us

profile of v3, /device:TPU:0, one launch (start us, length us, event | category | flops | bytes accessed | tf_op | source)
XLA Modules:
  0.0 32.6 jit_solution(128555029626887183)
XLA Ops:
  0.6 30.3 %shard_map.122 = (bf16[3,1,14,2816]{3,2,1,0:T(8,128)(2,1)S(1)}, bf16[16,16,896]{2,1,0:T(8,128)(2,1)S(1)}) custom-call(bf16[3,14,64,80]{3,2,1,0:T(8,128)(2,1)} %bitcast.6, bf16[3,1,14,2816]{3,2,1,0:T(8,128)(2,1)} %bitcast.7, bf16[1,1408,1280]{2,1,0:T(8,128)(2,1)} %leg_hbm.1, f32[28,28]{1,0:T(8,128)} %g_hbm.1, f32[28,28]{1,0:T(8,128)} %mi_hbm.1, ...), custom_call_target="tpu_custom_call" | custom-call | flops 1000000000 | bytes 8000000 | tf_op jit(solution)/shard_map/pallas_call | solution.py:481
  30.9 1.7 %shard_map.123 = (bf16[3,1,14,2816]{3,2,1,0:T(8,128)(2,1)}, bf16[3,14,64,80]{3,2,1,0:T(8,128)(2,1)}) custom-call(bf16[16,16,896]{2,1,0:T(8,128)(2,1)S(1)} %get-tuple-element.6.got, bf16[3,1,14,2816]{3,2,1,0:T(8,128)(2,1)S(1)} %get-tuple-element.7.spec_in), custom_call_target="tpu_custom_call" | custom-call | flops 200000000 | bytes 2000000 | tf_op jit(solution)/shard_map/pallas_call | solution.py:540

commit v4 on v3

--- a/solution.py
+++ b/solution.py
@@ -88,10 +88,10 @@
 
 def kernel(
     n, nlev, x_hbm, old_hbm, leg_hbm, g_hbm, mi_hbm, mo_hbm, mh_hbm, rates_hbm, pid_hbm, lat_hbm, lim_hbm,
-    spec_hbm, recv2,
-    spec_ref, x_ref, old_ref, leg, g_ref, mi_ref, mo_ref, mh_ref, rates_ref, pid_ref, lat_ref, lim_ref,
-    send1, recv1, send2, es, er, hot, turned,
-    out_sem, in_sem, s1, r1, s2, r2, es_sem, er_sem,
+    spec_ref, out_ref,
+    x_ref, old_ref, leg, g_ref, mi_ref, mo_ref, mh_ref, rates_ref, pid_ref, lat_ref, lim_ref,
+    send1, recv1, send2, recv2, es, er, hot, turned,
+    in_sem, s1, r1, s2, r2, es_sem, er_sem,
 ):
     lev_n = x_ref.shape[1]
     jl = x_ref.shape[3]
@@ -99,16 +99,6 @@
     nr, nlat = leg_hbm.shape[1:]
     me, lev = lax.axis_index("wave"), lax.axis_index("lev")
     other = lax.rem(lev + 1, nlev)
-    plane = n // 4
-    z, xy = me // plane, lax.rem(me, plane)
-    low = z < 2
-
-    def target(i):
-        zi, k = i // plane, lax.rem(i, plane)
-        far = jnp.where(low, 3 - zi, zi)
-        near = jnp.where(zi == 2, z + 1 - 2 * lax.rem(z, 2), z)
-        tz = jnp.where(zi < 2, far, near)
-        return tz * plane + lax.rem(xy + k + zi // 3, plane)
 
     pairs = [(x_hbm.at[f], x_ref.at[f]) for f in (0, 1, 2)] + [
         (pid_hbm, pid_ref), (lat_hbm, lat_ref), (lim_hbm, lim_ref), (g_hbm, g_ref), (mi_hbm, mi_ref),
@@ -117,10 +107,16 @@
     loads = [pltpu.make_async_copy(src, dst, in_sem.at[i]) for i, (src, dst) in enumerate(pairs)]
     for load in loads[:3]:
         load.start()
+    def away(i):
+        return lax.bitwise_xor(me, n - 1 - i)
+
+    def upwards(i):
+        return jnp.where(i < me, i, i + 1)
+
     barrier = pltpu.get_barrier_semaphore()
 
     def greet(i, carry):
-        pl.semaphore_signal(barrier, inc=1, device_id=(target(i), lev), device_id_type=MESH)
+        pl.semaphore_signal(barrier, inc=1, device_id=(upwards(i), lev), device_id_type=MESH)
         return carry
 
     lax.fori_loop(0, n - 1, greet, 0)
@@ -128,7 +124,7 @@
     for load in loads[3:]:
         load.start()
 
-    pr, pc = iota((CHUNK * 16, 4 * CHUNK * K), 0), iota((CHUNK * 16, 4 * CHUNK * K), 1)
+    pr, pc = iota((CHUNK * 16, 1), 0), iota((1, 4 * CHUNK * K), 1)
     home = pr % K * (4 * CHUNK) + pr // 16 * 4 + pr // 8 % 2 * 2
 
     def perm_of(g):
@@ -178,16 +174,12 @@
             device_id=(to, lev), device_id_type=MESH,
         )
 
-    def start_all(copy, p):
+    def start_all(copy, p, order):
         def start(i, carry):
-            copy(p, target(i)).start()
+            copy(p, order(i)).start()
             return carry
 
-        def start_up(i, carry):
-            copy(p, jnp.where(i < me, i, i + 1)).start()
-            return carry
-
-        lax.fori_loop(0, n - 1, start_up if copy is copy2 else start, 0)
+        lax.fori_loop(0, n - 1, start, 0)
 
     def whole(src, dst, bounds, ss, rr, p):
         at = pl.ds(bounds[p], bounds[p + 1] - bounds[p])
@@ -219,7 +211,7 @@
         done = last
         if p == 0:
             pl.semaphore_wait(barrier, n)
-        start_all(copy1, p)
+        start_all(copy1, p, away)
         recv1[me, :, lo:hi] = send1[me, :, lo:hi]
 
     for load in loads[3:12]:
@@ -344,7 +336,7 @@
 
     def send_piece(p):
         if down[p + 1] > down[p]:
-            start_all(copy2, p)
+            start_all(copy2, p, upwards)
 
     def arrive(p):
         if up[p + 1] > up[p]:
@@ -385,9 +377,6 @@
     send_piece(2)
     news = [vort, new1, new2]
 
-    own_copy = pltpu.make_async_copy(send2.at[me], recv2.at[me], out_sem.at[0])
-    own_copy.start()
-
     flat = [s for g in groups for s in g + [None] * (K - len(g))]
     starts = [e * K for e in ends]
 
@@ -408,64 +397,77 @@
                 l = stop
             rows = jnp.concatenate(parts, axis=0) if len(parts) > 1 else parts[0]
             spec_ref[f, 0, :, c * nr : (c + 1) * nr] = rows.astype(BF16)
-    spec_copy = pltpu.make_async_copy(spec_ref, spec_hbm, out_sem.at[1])
-    spec_copy.start()
+    qr, qc = iota((4 * CHUNK * K, 1), 0), iota((1, CHUNK * 16), 1)
+    q = qr % (4 * CHUNK)
+    home = q // 4 * 16 + q // 2 % 2 * 8 + qr // (4 * CHUNK)
+    backs = [onehot(qc == jnp.where(q % 2 == c, home, -1)) for c in range(2)]
+    where = {s: (g, k) for g, slots in enumerate(groups) for k, s in enumerate(slots)}
+    paired, single = [], []
+    for g, slots in enumerate(groups):
+        if all(c == 0 for f, l, c in slots):
+            b = where[slots[0][0], slots[0][1], 1][0]
+            if all(where[f, l, 1] == (b, k) for k, (f, l, c) in enumerate(slots)):
+                paired.append((g, b))
+    covered = {g for pair in paired for g in pair}
+    for g, slots in enumerate(groups):
+        if g not in covered:
+            zero = [(f, l) for f, l, c in slots if c == 0]
+            count = len(zero)
+            sr = iota((4 * CHUNK * count, 1), 0)
+            sq = sr % (4 * CHUNK)
+            single.append(
+                (g, zero, onehot(qc == sq // 4 * 16 + sq // 2 % 2 * 8 + sr // (4 * CHUNK) + count * (sq % 2)))
+            )
+
+    def stage(g):
+        return min(p for p in range(3) if base[g] + jl <= down[p + 1])
+
+    def wide(p, h, run):
+        rows = recv2[h * CHUNK : (h + 1) * CHUNK, :, : down[p + 1]].reshape(CHUNK * 16, down[p + 1])
+        rows = [rows[:, base[g] : base[g] + jl] for g in run]
+        return jnp.concatenate(rows, axis=1) if len(rows) > 1 else rows[0]
+
+    tops = {}
+    for p in range(3):
+        lo, hi = down[p], down[p + 1]
+        if hi > lo:
+            recv2[me, :, lo:hi] = send2[me, :, lo:hi]
+            whole(send2, recv2, down, s2, r2, p).wait_recv()
+        now = [(g, b) for g, b in paired if max(stage(g), stage(b)) == p]
+        half_now = [g for g, b in paired if stage(g) == p]
+        for h in range(n // CHUNK):
+            qs = slice(h * 4 * CHUNK, (h + 1) * 4 * CHUNK)
+            if half_now:
+                got = dot(backs[0], wide(p, h, half_now))
+                tops.update({(h, g): got[:, i * jl : (i + 1) * jl] for i, g in enumerate(half_now)})
+            if now:
+                got = dot(backs[1], wide(p, h, [b for g, b in now]))
+                for i, (g, b) in enumerate(now):
+                    piece = (got[:, i * jl : (i + 1) * jl] + tops[h, g]).astype(BF16)
+                    for k, (f, l, c) in enumerate(groups[g]):
+                        out_ref[f, l, qs] = piece[k * 4 * CHUNK : (k + 1) * 4 * CHUNK]
+            for g, zero, perm in single:
+                if stage(g) == p:
+                    piece = dot(perm, wide(p, h, [g])).astype(BF16)
+                    for k, (f, l) in enumerate(zero):
+                        out_ref[f, l, qs] = piece[k * 4 * CHUNK : (k + 1) * 4 * CHUNK]
 
     for p in range(3):
         if up[p + 1] > up[p]:
             whole(send1, recv1, up, s1, r1, p).wait_send()
         if down[p + 1] > down[p]:
             whole(send2, recv2, down, s2, r2, p).wait_send()
-    own_copy.wait()
-    spec_copy.wait()
-    for p in range(3):
-        if down[p + 1] > down[p]:
-            whole(send2, recv2, down, s2, r2, p).wait_recv()
-
-
-def finish(n, lev_n, jl, got, spec_in, spec_hbm, out_hbm, out_ref, sem):
-    groups, ends, lanes, base, up, down = make_pieces(lev_n, jl)
-    spec_copy = pltpu.make_async_copy(spec_in, spec_hbm, sem.at[3])
-    spec_copy.start()
-    where = {s: (g, k) for g, slots in enumerate(groups) for k, s in enumerate(slots)}
-    pr, pc = iota((4 * CHUNK * K, 2 * CHUNK * 16), 0), iota((4 * CHUNK * K, 2 * CHUNK * 16), 1)
-    q = pr % (4 * CHUNK)
-    perm = onehot(pc == q % 2 * (CHUNK * 16) + q // 4 * 16 + q // 2 % 2 * 8 + pr // (4 * CHUNK))
-    paired, single = [], {}
-    for g, slots in enumerate(groups):
-        partners = {where[(f, l, 1)] for f, l, c in slots if c == 0}
-        if all(c == 0 for f, l, c in slots) and len({b for b, k in partners}) == 1:
-            b = next(iter(partners))[0]
-            if all(where[(f, l, 1)] == (b, k) for k, (f, l, c) in enumerate(slots)):
-                paired.append((g, b))
-    covered = {g for pair in paired for g in pair}
-    for g, slots in enumerate(groups):
-        if g not in covered:
-            single[g] = slots
-    for h in range(n // CHUNK):
-        rows = got[h * CHUNK : (h + 1) * CHUNK].reshape(CHUNK * 16, lanes)
-        qs = slice(h * 4 * CHUNK, (h + 1) * 4 * CHUNK)
-        tops = jnp.concatenate([rows[:, base[g] : base[g] + jl] for g, b in paired], axis=1)
-        bots = jnp.concatenate([rows[:, base[b] : base[b] + jl] for g, b in paired], axis=1)
-        back = dot(perm, jnp.concatenate([tops, bots], axis=0)).astype(BF16)
-        for i, (g, b) in enumerate(paired):
-            for k, (f, l, c) in enumerate(groups[g]):
-                out_ref[f, l, qs] = back[k * 4 * CHUNK : (k + 1) * 4 * CHUNK, i * jl : (i + 1) * jl]
-        for g, slots in single.items():
-            zero = [(f, l) for f, l, c in slots if c == 0]
-            count = len(zero)
-            sr, sc = iota((4 * CHUNK * count, CHUNK * 16), 0), iota((4 * CHUNK * count, CHUNK * 16), 1)
-            sq, sk = sr % (4 * CHUNK), sr // (4 * CHUNK)
-            some = onehot(sc == sq // 4 * 16 + sq // 2 % 2 * 8 + sk + count * (sq % 2))
-            back = dot(some, rows[:, base[g] : base[g] + jl]).astype(BF16)
-            for k, (f, l) in enumerate(zero):
-                out_ref[f, l, qs] = back[k * 4 * CHUNK : (k + 1) * 4 * CHUNK]
-    copies = [pltpu.make_async_copy(out_ref.at[f], out_hbm.at[f], sem.at[f]) for f in range(3)]
+
+
+def finish(spec, out, spec_hbm, out_hbm, sem):
+    copies = [
+        pltpu.make_async_copy(out, out_hbm, sem.at[0]),
+        pltpu.make_async_copy(spec, spec_hbm, sem.at[1]),
+    ]
     for copy in copies:
         copy.start()
     for copy in copies:
         copy.wait()
-    spec_copy.wait()
 
 
 def body(
@@ -478,16 +480,16 @@
     nr, nlat = legendre.shape[1:]
     half = (nlev * lev_n + 15) // 16 * 16
     hbm = pl.BlockSpec(memory_space=pltpu.HBM)
-    spec, got = pl.pallas_call(
+    vmem = pl.BlockSpec(memory_space=pltpu.VMEM)
+    spec, out = pl.pallas_call(
         functools.partial(kernel, n, nlev),
         out_shape=(
             jax.ShapeDtypeStruct((fields, 1, lev_n, 2 * nr), BF16),
-            jax.ShapeDtypeStruct((n, 16, lanes), BF16),
+            jax.ShapeDtypeStruct((fields, lev_n, q_n, jl), BF16),
         ),
         in_specs=[hbm] * 11,
-        out_specs=(hbm, hbm),
+        out_specs=(vmem, vmem),
         scratch_shapes=[
-            pltpu.VMEM((fields, 1, lev_n, 2 * nr), BF16),
             pltpu.VMEM((fields, lev_n, q_n, jl), BF16),
             pltpu.VMEM((fields, 1, lev_n, 2 * nr), BF16),
             pltpu.VMEM((nr, nlat), BF16),
@@ -502,11 +504,11 @@
             pltpu.VMEM((n, 16, lanes), BF16),
             pltpu.VMEM((n, 16, lanes), BF16),
             pltpu.VMEM((n, 16, lanes), BF16),
+            pltpu.VMEM((n, 16, lanes), BF16),
             pltpu.VMEM((2, half, nr), BF16),
             pltpu.VMEM((2, half, nr), BF16),
             pltpu.VMEM((nlat, nlat), BF16),
             pltpu.VMEM((nlat, nr), BF16),
-            pltpu.SemaphoreType.DMA((2,)),
             pltpu.SemaphoreType.DMA((13,)),
             pltpu.SemaphoreType.DMA((3,)),
             pltpu.SemaphoreType.DMA((3,)),
@@ -538,20 +540,17 @@
         ]
     )
     spec, out = pl.pallas_call(
-        functools.partial(finish, n, lev_n, jl),
+        finish,
         out_shape=(
-            jax.ShapeDtypeStruct((fields, 1, lev_n, 2 * nr), BF16),
-            jax.ShapeDtypeStruct((fields, lev_n, q_n, jl), BF16),
+            jax.ShapeDtypeStruct(spec.shape, BF16),
+            jax.ShapeDtypeStruct(out.shape, BF16),
         ),
-        in_specs=[pl.BlockSpec(memory_space=pltpu.VMEM)] * 2,
+        in_specs=[vmem] * 2,
         out_specs=(hbm, hbm),
-        scratch_shapes=[
-            pltpu.VMEM((fields, lev_n, q_n, jl), BF16),
-            pltpu.SemaphoreType.DMA((4,)),
-        ],
+        scratch_shapes=[pltpu.SemaphoreType.DMA((2,))],
         compiler_params=pltpu.CompilerParams(vmem_limit_bytes=48 * 1024 * 1024),
-        cost_estimate=pl.CostEstimate(flops=2 * 10**8, bytes_accessed=2 * 10**6, transcendentals=0),
-    )(got, spec)
+        cost_estimate=pl.CostEstimate(flops=0, bytes_accessed=2 * 10**6, transcendentals=0),
+    )(spec, out)
     return jnp.transpose(spec, (0, 2, 1, 3)), jnp.transpose(out, (0, 1, 3, 2))
 
 

time: 32.7 us -> 31 us (0.948)
  Pallas kernels: 32 us -> 30.2 us
    pallas_call x1, Pallas kernels: 30.3 us -> 29.3 us  [body(): pl.pallas_call(functools.partial(kernel, n, nlev), out_shape=(jax.ShapeDt...]
    pallas_call x1, Pallas kernels: 1.68 us -> 0.95 us  [body(): pl.pallas_call(finish, out_shape=(jax.ShapeDtypeStruct(spec.shape, BF16),...]
where the time goes in v4:
time: 31 us; the launch traced here: 30.8 us
  Pallas kernels  30.2 us (97%)
  between operations  0.64 us (2%)
    pallas_call x1, Pallas kernels, body(): pl.pallas_call(functools.partial(kernel, n, nlev), out_shape=(jax.ShapeDt...  29.3 us
    pallas_call x1, Pallas kernels, body(): pl.pallas_call(finish, out_shape=(jax.ShapeDtypeStruct(spec.shape, BF16),...  0.95 us

profile of v4, /device:TPU:0, one launch (start us, length us, event | category | flops | bytes accessed | tf_op | source)
XLA Modules:
  0.0 30.8 jit_solution(9857659543167807271)
XLA Ops:
  0.6 29.3 %shard_map.122 = (bf16[3,1,14,2816]{3,2,1,0:T(8,128)(2,1)S(1)}, bf16[3,14,64,80]{3,2,1,0:T(8,128)(2,1)S(1)}) custom-call(bf16[3,14,64,80]{3,2,1,0:T(8,128)(2,1)} %bitcast.6, bf16[3,1,14,2816]{3,2,1,0:T(8,128)(2,1)} %bitcast.7, bf16[1,1408,1280]{2,1,0:T(8,128)(2,1)} %leg_hbm.1, f32[28,28]{1,0:T(8,128)} %g_hbm.1, f32[28,28]{1,0:T(8,128)} %mi_hbm.1, ...), custom_call_target="tpu_custom_call" | custom-call | flops 1000000000 | bytes 8000000 | tf_op jit(solution)/shard_map/pallas_call | solution.py:484
  29.9 1.0 %shard_map.123 = (bf16[3,1,14,2816]{3,2,1,0:T(8,128)(2,1)}, bf16[3,14,64,80]{3,2,1,0:T(8,128)(2,1)}) custom-call(bf16[3,1,14,2816]{3,2,1,0:T(8,128)(2,1)S(1)} %get-tuple-element.6.spec, bf16[3,14,64,80]{3,2,1,0:T(8,128)(2,1)S(1)} %get-tuple-element.7.out), custom_call_target="tpu_custom_call" | custom-call | bytes 2000000 | tf_op jit(solution)/shard_map/pallas_call | solution.py:542

commit v5 on v4

--- a/solution.py
+++ b/solution.py
@@ -108,7 +108,7 @@
     for load in loads[:3]:
         load.start()
     def away(i):
-        return lax.bitwise_xor(me, n - 1 - i)
+        return lax.bitwise_xor(me, jnp.where(i % 2 == 0, n - 1 - i // 2, 1 + i // 2))
 
     def upwards(i):
         return jnp.where(i < me, i, i + 1)

time: 31 us -> 30.6 us (0.987)
  Pallas kernels: 30.2 us -> 29.8 us
    pallas_call x1, Pallas kernels: 29.3 us -> 28.8 us  [body(): pl.pallas_call(functools.partial(kernel, n, nlev), out_shape=(jax.ShapeDt...]
where the time goes in v5:
time: 30.6 us; the launch traced here: 30.4 us
  Pallas kernels  29.8 us (97%)
  between operations  0.64 us (2%)
    pallas_call x1, Pallas kernels, body(): pl.pallas_call(functools.partial(kernel, n, nlev), out_shape=(jax.ShapeDt...  28.8 us
    pallas_call x1, Pallas kernels, body(): pl.pallas_call(finish, out_shape=(jax.ShapeDtypeStruct(spec.shape, BF16),...  0.95 us

profile of v5, /device:TPU:0, one launch (start us, length us, event | category | flops | bytes accessed | tf_op | source)
XLA Modules:
  0.0 30.4 jit_solution(1699228529066944353)
XLA Ops:
  0.6 28.8 %shard_map.122 = (bf16[3,1,14,2816]{3,2,1,0:T(8,128)(2,1)S(1)}, bf16[3,14,64,80]{3,2,1,0:T(8,128)(2,1)S(1)}) custom-call(bf16[3,14,64,80]{3,2,1,0:T(8,128)(2,1)} %bitcast.6, bf16[3,1,14,2816]{3,2,1,0:T(8,128)(2,1)} %bitcast.7, bf16[1,1408,1280]{2,1,0:T(8,128)(2,1)} %leg_hbm.1, f32[28,28]{1,0:T(8,128)} %g_hbm.1, f32[28,28]{1,0:T(8,128)} %mi_hbm.1, ...), custom_call_target="tpu_custom_call" | custom-call | flops 1000000000 | bytes 8000000 | tf_op jit(solution)/shard_map/pallas_call | solution.py:484
  29.5 1.0 %shard_map.123 = (bf16[3,1,14,2816]{3,2,1,0:T(8,128)(2,1)}, bf16[3,14,64,80]{3,2,1,0:T(8,128)(2,1)}) custom-call(bf16[3,1,14,2816]{3,2,1,0:T(8,128)(2,1)S(1)} %get-tuple-element.6.spec, bf16[3,14,64,80]{3,2,1,0:T(8,128)(2,1)S(1)} %get-tuple-element.7.out), custom_call_target="tpu_custom_call" | custom-call | bytes 2000000 | tf_op jit(solution)/shard_map/pallas_call | solution.py:542

commit v6 on v5

--- a/solution.py
+++ b/solution.py
@@ -107,8 +107,10 @@
     loads = [pltpu.make_async_copy(src, dst, in_sem.at[i]) for i, (src, dst) in enumerate(pairs)]
     for load in loads[:3]:
         load.start()
+    plane = n // 4
+
     def away(i):
-        return lax.bitwise_xor(me, jnp.where(i % 2 == 0, n - 1 - i // 2, 1 + i // 2))
+        return lax.bitwise_xor(me, jnp.where((lev == 0) & (i % 2 == 0), n - 1 - i // 2, jnp.where(lev == 0, 1 + i // 2, n - 1 - i)))
 
     def upwards(i):
         return jnp.where(i < me, i, i + 1)
@@ -170,7 +172,7 @@
     def copy2(p, to):
         at = pl.ds(down[p], down[p + 1] - down[p])
         return pltpu.make_async_remote_copy(
-            src_ref=send2.at[to, :, at], dst_ref=recv2.at[me, :, at], send_sem=s2.at[p], recv_sem=r2.at[p],
+            src_ref=send2.at[to, :, at], dst_ref=recv2.at[me, :, at], send_sem=s2.at[p], recv_sem=r2.at[p + me // plane if p == 2 else p],
             device_id=(to, lev), device_id_type=MESH,
         )
 
@@ -336,7 +338,7 @@
 
     def send_piece(p):
         if down[p + 1] > down[p]:
-            start_all(copy2, p, upwards)
+            start_all(copy2, p, upwards if p else away)
 
     def arrive(p):
         if up[p + 1] > up[p]:
@@ -427,23 +429,18 @@
         rows = [rows[:, base[g] : base[g] + jl] for g in run]
         return jnp.concatenate(rows, axis=1) if len(rows) > 1 else rows[0]
 
-    tops = {}
-    for p in range(3):
+    for p in range(2):
         lo, hi = down[p], down[p + 1]
         if hi > lo:
             recv2[me, :, lo:hi] = send2[me, :, lo:hi]
             whole(send2, recv2, down, s2, r2, p).wait_recv()
         now = [(g, b) for g, b in paired if max(stage(g), stage(b)) == p]
-        half_now = [g for g, b in paired if stage(g) == p]
         for h in range(n // CHUNK):
             qs = slice(h * 4 * CHUNK, (h + 1) * 4 * CHUNK)
-            if half_now:
-                got = dot(backs[0], wide(p, h, half_now))
-                tops.update({(h, g): got[:, i * jl : (i + 1) * jl] for i, g in enumerate(half_now)})
             if now:
-                got = dot(backs[1], wide(p, h, [b for g, b in now]))
+                got = dot(backs[0], wide(p, h, [g for g, b in now])) + dot(backs[1], wide(p, h, [b for g, b in now]))
                 for i, (g, b) in enumerate(now):
-                    piece = (got[:, i * jl : (i + 1) * jl] + tops[h, g]).astype(BF16)
+                    piece = got[:, i * jl : (i + 1) * jl].astype(BF16)
                     for k, (f, l, c) in enumerate(groups[g]):
                         out_ref[f, l, qs] = piece[k * 4 * CHUNK : (k + 1) * 4 * CHUNK]
             for g, zero, perm in single:
@@ -457,6 +454,31 @@
             whole(send1, recv1, up, s1, r1, p).wait_send()
         if down[p + 1] > down[p]:
             whole(send2, recv2, down, s2, r2, p).wait_send()
+
+    lo, hi = down[2], down[3]
+    recv2[me, :, lo:hi] = send2[me, :, lo:hi]
+    now = [(g, b) for g, b in paired if max(stage(g), stage(b)) == 2]
+    wide_q = 4 * plane
+    qr, qc = iota((wide_q * K, 1), 0), iota((1, 2 * plane * 16), 1)
+    q = qr % wide_q
+    turn_back = onehot(qc == q % 2 * (plane * 16) + q // 4 * 16 + q // 2 % 2 * 8 + qr // wide_q)
+    for i in range(4):
+        t = lax.bitwise_xor(me // plane, i)
+        count = plane if i else plane - 1
+        landed = recv2.at[pl.ds(0, count), :, pl.ds(lo, hi - lo)]
+        pltpu.make_async_remote_copy(
+            src_ref=send2.at[pl.ds(0, count), :, pl.ds(lo, hi - lo)], dst_ref=landed, send_sem=s2.at[2],
+            recv_sem=r2.at[2 + t], device_id=(me, other), device_id_type=MESH,
+        ).wait_recv()
+        rows = recv2[pl.ds(t * plane, plane)].reshape(plane * 16, lanes)
+        data = [
+            jnp.concatenate([rows[:, base[g] : base[g] + jl] for g in run], axis=1) for run in zip(*now)
+        ]
+        got = dot(turn_back, jnp.concatenate(data, axis=0)).astype(BF16)
+        at = pl.ds(pl.multiple_of(t * wide_q, wide_q), wide_q)
+        for m, (g, b) in enumerate(now):
+            for k, (f, l, c) in enumerate(groups[g]):
+                out_ref[f, l, at] = got[k * wide_q : (k + 1) * wide_q, m * jl : (m + 1) * jl]
 
 
 def finish(spec, out, spec_hbm, out_hbm, sem):
@@ -513,7 +535,7 @@
             pltpu.SemaphoreType.DMA((3,)),
             pltpu.SemaphoreType.DMA((3,)),
             pltpu.SemaphoreType.DMA((3,)),
-            pltpu.SemaphoreType.DMA((3,)),
+            pltpu.SemaphoreType.DMA((6,)),
             pltpu.SemaphoreType.DMA((2,)),
             pltpu.SemaphoreType.DMA((2,)),
         ],

time: 30.6 us -> 30.5 us (level)
  no operation moved by 1% of the time
where the time goes in v6:
time: 30.5 us; the launch traced here: 30.3 us
  Pallas kernels  29.7 us (97%)
  between operations  0.64 us (2%)
    pallas_call x1, Pallas kernels, body(): pl.pallas_call(functools.partial(kernel, n, nlev), out_shape=(jax.ShapeDt...  28.8 us
    pallas_call x1, Pallas kernels, body(): pl.pallas_call(finish, out_shape=(jax.ShapeDtypeStruct(spec.shape, BF16),...  0.95 us

profile of v6, /device:TPU:0, one launch (start us, length us, event | category | flops | bytes accessed | tf_op | source)
XLA Modules:
  0.0 30.3 jit_solution(16155093492919232184)
XLA Ops:
  0.6 28.8 %shard_map.122 = (bf16[3,1,14,2816]{3,2,1,0:T(8,128)(2,1)S(1)}, bf16[3,14,64,80]{3,2,1,0:T(8,128)(2,1)S(1)}) custom-call(bf16[3,14,64,80]{3,2,1,0:T(8,128)(2,1)} %bitcast.6, bf16[3,1,14,2816]{3,2,1,0:T(8,128)(2,1)} %bitcast.7, bf16[1,1408,1280]{2,1,0:T(8,128)(2,1)} %leg_hbm.1, f32[28,28]{1,0:T(8,128)} %g_hbm.1, f32[28,28]{1,0:T(8,128)} %mi_hbm.1, ...), custom_call_target="tpu_custom_call" | custom-call | flops 1000000000 | bytes 8000000 | tf_op jit(solution)/shard_map/pallas_call | solution.py:506
  29.4 1.0 %shard_map.123 = (bf16[3,1,14,2816]{3,2,1,0:T(8,128)(2,1)}, bf16[3,14,64,80]{3,2,1,0:T(8,128)(2,1)}) custom-call(bf16[3,1,14,2816]{3,2,1,0:T(8,128)(2,1)S(1)} %get-tuple-element.6.spec, bf16[3,14,64,80]{3,2,1,0:T(8,128)(2,1)S(1)} %get-tuple-element.7.out), custom_call_target="tpu_custom_call" | custom-call | bytes 2000000 | tf_op jit(solution)/shard_map/pallas_call | solution.py:564

commit v7 on v6

--- a/solution.py
+++ b/solution.py
@@ -165,14 +165,14 @@
     def copy1(p, to):
         at = pl.ds(up[p], up[p + 1] - up[p])
         return pltpu.make_async_remote_copy(
-            src_ref=send1.at[to, :, at], dst_ref=recv1.at[me, :, at], send_sem=s1.at[p], recv_sem=r1.at[p],
+            src_ref=send1.at[to, :, at], dst_ref=recv1.at[me, :, at], send_sem=s1.at[0], recv_sem=r1.at[p],
             device_id=(to, lev), device_id_type=MESH,
         )
 
     def copy2(p, to):
         at = pl.ds(down[p], down[p + 1] - down[p])
         return pltpu.make_async_remote_copy(
-            src_ref=send2.at[to, :, at], dst_ref=recv2.at[me, :, at], send_sem=s2.at[p], recv_sem=r2.at[p + me // plane if p == 2 else p],
+            src_ref=send2.at[to, :, at], dst_ref=recv2.at[me, :, at], send_sem=s2.at[0], recv_sem=r2.at[p + me // plane if p == 2 else p],
             device_id=(to, lev), device_id_type=MESH,
         )
 
@@ -186,7 +186,7 @@
     def whole(src, dst, bounds, ss, rr, p):
         at = pl.ds(bounds[p], bounds[p + 1] - bounds[p])
         return pltpu.make_async_remote_copy(
-            src_ref=src.at[pl.ds(0, n - 1), :, at], dst_ref=dst.at[pl.ds(0, n - 1), :, at], send_sem=ss.at[p],
+            src_ref=src.at[pl.ds(0, n - 1), :, at], dst_ref=dst.at[pl.ds(0, n - 1), :, at], send_sem=ss.at[0],
             recv_sem=rr.at[p], device_id=(me, other), device_id_type=MESH,
         )
 
@@ -449,11 +449,8 @@
                     for k, (f, l) in enumerate(zero):
                         out_ref[f, l, qs] = piece[k * 4 * CHUNK : (k + 1) * 4 * CHUNK]
 
-    for p in range(3):
-        if up[p + 1] > up[p]:
-            whole(send1, recv1, up, s1, r1, p).wait_send()
-        if down[p + 1] > down[p]:
-            whole(send2, recv2, down, s2, r2, p).wait_send()
+    whole(send1, recv1, [0, lanes], s1, r1, 0).wait_send()
+    whole(send2, recv2, [0, lanes], s2, r2, 0).wait_send()
 
     lo, hi = down[2], down[3]
     recv2[me, :, lo:hi] = send2[me, :, lo:hi]
@@ -467,7 +464,7 @@
         count = plane if i else plane - 1
         landed = recv2.at[pl.ds(0, count), :, pl.ds(lo, hi - lo)]
         pltpu.make_async_remote_copy(
-            src_ref=send2.at[pl.ds(0, count), :, pl.ds(lo, hi - lo)], dst_ref=landed, send_sem=s2.at[2],
+            src_ref=send2.at[pl.ds(0, count), :, pl.ds(lo, hi - lo)], dst_ref=landed, send_sem=s2.at[0],
             recv_sem=r2.at[2 + t], device_id=(me, other), device_id_type=MESH,
         ).wait_recv()
         rows = recv2[pl.ds(t * plane, plane)].reshape(plane * 16, lanes)
@@ -532,9 +529,9 @@
             pltpu.VMEM((nlat, nlat), BF16),
             pltpu.VMEM((nlat, nr), BF16),
             pltpu.SemaphoreType.DMA((13,)),
+            pltpu.SemaphoreType.DMA((1,)),
             pltpu.SemaphoreType.DMA((3,)),
-            pltpu.SemaphoreType.DMA((3,)),
-            pltpu.SemaphoreType.DMA((3,)),
+            pltpu.SemaphoreType.DMA((1,)),
             pltpu.SemaphoreType.DMA((6,)),
             pltpu.SemaphoreType.DMA((2,)),
             pltpu.SemaphoreType.DMA((2,)),

time: 30.5 us -> 30.5 us (level)
  no operation moved by 1% of the time
where the time goes in v7:
time: 30.5 us; the launch traced here: 30.3 us
  Pallas kernels  29.7 us (97%)
  between operations  0.64 us (2%)
    pallas_call x1, Pallas kernels, body(): pl.pallas_call(functools.partial(kernel, n, nlev), out_shape=(jax.ShapeDt...  28.7 us
    pallas_call x1, Pallas kernels, body(): pl.pallas_call(finish, out_shape=(jax.ShapeDtypeStruct(spec.shape, BF16),...  0.95 us

profile of v7, /device:TPU:0, one launch (start us, length us, event | category | flops | bytes accessed | tf_op | source)
XLA Modules:
  0.0 30.3 jit_solution(11035856497506675739)
XLA Ops:
  0.6 28.7 %shard_map.122 = (bf16[3,1,14,2816]{3,2,1,0:T(8,128)(2,1)S(1)}, bf16[3,14,64,80]{3,2,1,0:T(8,128)(2,1)S(1)}) custom-call(bf16[3,14,64,80]{3,2,1,0:T(8,128)(2,1)} %bitcast.6, bf16[3,1,14,2816]{3,2,1,0:T(8,128)(2,1)} %bitcast.7, bf16[1,1408,1280]{2,1,0:T(8,128)(2,1)} %leg_hbm.1, f32[28,28]{1,0:T(8,128)} %g_hbm.1, f32[28,28]{1,0:T(8,128)} %mi_hbm.1, ...), custom_call_target="tpu_custom_call" | custom-call | flops 1000000000 | bytes 8000000 | tf_op jit(solution)/shard_map/pallas_call | solution.py:503
  29.4 1.0 %shard_map.123 = (bf16[3,1,14,2816]{3,2,1,0:T(8,128)(2,1)}, bf16[3,14,64,80]{3,2,1,0:T(8,128)(2,1)}) custom-call(bf16[3,1,14,2816]{3,2,1,0:T(8,128)(2,1)S(1)} %get-tuple-element.6.spec, bf16[3,14,64,80]{3,2,1,0:T(8,128)(2,1)S(1)} %get-tuple-element.7.out), custom_call_target="tpu_custom_call" | custom-call | bytes 2000000 | tf_op jit(solution)/shard_map/pallas_call | solution.py:561
